TPU v7x, 256 devices: a whole 4x4x8 slice. The times are simulated.
256 devices in a mesh: tm: 64 (over x, z, core), items: 4 (over y).
Axes of the slice: x: 4, y: 4, z: 8, core: 2. Of those that a mesh axis runs over, the one named last changes fastest.
Arguments:
- production: float32 [3072, 16384], P('tm', 'items'), may hold values from 0 to 2
- setup: float32 [3072, 16384], P('tm', 'items'), may hold values from 0 to 1
- shortage: float32 [3072, 16384], P('tm', 'items'), may hold values from 0 to 1
- dual_demand: float32 [3072, 16384], P('tm', 'items'), may hold values from 0.05 to 2
- dual_link: float32 [3072, 16384], P('tm', 'items'), may hold values from 0.05 to 1
- dual_resource: float32 [3072, 128], P('tm'), may hold values from 0.05 to 1
- cost_production: float32 [3072, 16384], P('tm', 'items'), may hold values from 0.1 to 2
- cost_setup: float32 [16384], P('items'), may hold values from 0.5 to 4
- penalty: float32 [16384], P('items'), may hold values from 1 to 8
- demand: float32 [3072, 16384], P('tm', 'items'), may hold values from 0.2 to 1.5
- capacity: float32 [3072, 128], P('tm'), may hold values from 12.8 to 64
- coef_production: float32 [256, 128], replicated, may hold values from 0.0015625 to 0.015625
- coef_setup: float32 [256, 128], replicated, may hold values from 0.0015625 to 0.015625
- horizon_start: int32 [16384], P('items'), may hold values from 0 to 3071, as said below
- horizon_end: int32 [16384], P('items'), may hold values from 0 to 3071, as said below
- fixing: int32 [3072, 16384], P('tm', 'items'), may hold values from 0 to 2
- block_id: int32 [16384], P('items'), may hold values from 0 to 255
Outputs:
- production_next: float32 [3072, 16384], P('tm', 'items')
- setup_next: float32 [3072, 16384], P('tm', 'items')
- shortage_next: float32 [3072, 16384], P('tm', 'items')
- dual_demand_next: float32 [3072, 16384], P('tm', 'items')
- dual_link_next: float32 [3072, 16384], P('tm', 'items')
- dual_resource_next: float32 [3072, 128], P('tm')
Inputs may be any that keep to these rules, and one draw needn't show every extreme that they name: horizon_start[i] <= horizon_end[i] for every item; some item's horizon starts in the first period. `horizon_end`: some item's horizon ends in the last period.
All inputs are finite; a program needn't handle non-finite values.
Results may differ from a plain program's by a relative error of at most 0.00007.
Values sent between devices are 32-bit elements; how exact they have to be, the bound alone decides.
A program may use at most 64 MiB of HBM per device.

v0:
```python
import functools

import jax
import jax.numpy as jnp
from jax import lax
from jax.experimental import pallas as pl
from jax.experimental.pallas import tpu as pltpu
from jax.sharding import PartitionSpec as P

MESH = pl.DeviceIdType.MESH
F32 = jnp.float32
BF16 = jnp.bfloat16

big_m = 4.0
setup_step = 0.5
short_step = 0.5
link_step = 0.25

LANES = 128
GROUP = 8
CORES = 2
DEPTH = 8


def suffix_rows(groups, sub):
    tail = jnp.zeros((GROUP, LANES), F32)
    out = [None] * len(groups)
    for g in reversed(range(len(groups))):
        part = groups[g]
        for shift in (1, 2, 4):
            moved = pltpu.roll(part, GROUP - shift, 0)
            part = part + jnp.where(sub < GROUP - shift, moved, 0.0)
        out[g] = part + tail
        tail = jnp.broadcast_to(out[g][0:1, :], (GROUP, LANES))
    return out, tail


def prefix_rows(groups, sub):
    head = jnp.zeros((GROUP, LANES), F32)
    out = [None] * len(groups)
    for g in range(len(groups)):
        part = groups[g]
        for shift in (1, 2, 4):
            moved = pltpu.roll(part, shift, 0)
            part = part + jnp.where(sub >= shift, moved, 0.0)
        out[g] = part + head
        head = jnp.broadcast_to(out[g][GROUP - 1 :, :], (GROUP, LANES))
    return out


def halves(value, count):
    terms = []
    for k in range(count):
        term = value.astype(BF16)
        terms.append(term)
        if k + 1 < count:
            value = value - term.astype(F32)
    return terms


def exact(left, right, contract):
    return lax.dot_general(
        left, right, (contract, ((), ())), precision=lax.Precision.HIGHEST, preferred_element_type=F32
    )


def kernel(
    ranks,
    items_total,
    production_h,
    setup_h,
    shortage_h,
    dual_demand_h,
    dual_link_h,
    dual_resource_h,
    cost_production_h,
    cost_setup_h,
    penalty_h,
    demand_h,
    capacity_h,
    coef_production_h,
    coef_setup_h,
    start_h,
    end_h,
    fixing_h,
    block_h,
    production_o,
    setup_o,
    shortage_o,
    dual_demand_o,
    dual_link_o,
    dual_resource_o,
    production_v,
    setup_v,
    shortage_v,
    dual_demand_v,
    dual_link_v,
    cost_production_v,
    demand_v,
    fixing_v,
    dual_resource_v,
    capacity_v,
    coef_production_v,
    coef_setup_v,
    cost_setup_v,
    penalty_v,
    start_v,
    end_v,
    block_v,
    start_f,
    end_f,
    onehot_v,
    pull_production_v,
    pull_setup_v,
    local_v,
    primal_step_v,
    dual_step_v,
    setup_bar_v,
    prod_bar_v,
    link_v,
    flow_v,
    own_v,
    sibling_v,
    along_z_v,
    along_x_v,
    inside_v,
    carry_v,
    usage_v,
    in_sem,
    out_sem,
    core_send,
    core_recv,
    z_send,
    z_recv,
    x_send,
    x_recv,
    inside_send,
    inside_recv,
    y_send,
    y_recv,
):
    nx, nz, ny = ranks
    rows, items = production_v.shape
    groups = rows // GROUP
    chunks = items // LANES
    half = chunks // 2
    blocks = coef_production_v.shape[0]
    tm = lax.axis_index("tm")
    y = lax.axis_index("items")
    core = lax.rem(tm, CORES)
    z = lax.rem(tm // CORES, nz)
    x = tm // (CORES * nz)

    def place(px, pz, pc, py=None):
        return ((px * nz + pz) * CORES + pc, y if py is None else py)

    loads = [
        (start_h, start_v),
        (end_h, end_v),
        (dual_demand_h, dual_demand_v),
        (block_h, block_v),
        (dual_resource_h, dual_resource_v),
        (coef_production_h, coef_production_v),
        (coef_setup_h, coef_setup_v),
        (cost_setup_h, cost_setup_v),
        (penalty_h, penalty_v),
        (dual_link_h, dual_link_v),
        (setup_h, setup_v),
        (fixing_h, fixing_v),
        (shortage_h, shortage_v),
        (production_h, production_v),
        (cost_production_h, cost_production_v),
        (demand_h, demand_v),
        (capacity_h, capacity_v),
    ]
    load = [pltpu.make_async_copy(src, dst, in_sem.at[k]) for k, (src, dst) in enumerate(loads)]
    for copy in load:
        copy.start()

    barrier = pltpu.get_barrier_semaphore()
    greeted = 0
    for d in range(1, nz):
        pl.semaphore_signal(
            barrier, inc=1, device_id=place(x, lax.rem(z + d, nz), core), device_id_type=MESH
        )
        greeted += 1
    for d in range(1, nx):
        for c in range(CORES):
            pl.semaphore_signal(
                barrier, inc=1, device_id=place(lax.rem(x + d, nx), z, c), device_id_type=MESH
            )
            greeted += 1
    for d in range(1, ny):
        pl.semaphore_signal(
            barrier, inc=1, device_id=place(x, z, core, lax.rem(y + d, ny)), device_id_type=MESH
        )
        greeted += 1
    pl.semaphore_signal(barrier, inc=1, device_id=place(x, z, 1 - core), device_id_type=MESH)
    greeted += 1

    sub = lax.broadcasted_iota(jnp.int32, (GROUP, LANES), 0)
    first = (tm * rows).astype(F32)
    period = [sub.astype(F32) + (first + float(g * GROUP)) for g in range(groups)]

    def lanes(j):
        return pl.ds(pl.multiple_of(j * LANES, LANES), LANES)

    def piece(ref, g, j):
        return ref[g * GROUP : (g + 1) * GROUP, lanes(j)]

    def put(ref, g, j, value):
        ref[g * GROUP : (g + 1) * GROUP, lanes(j)] = value

    def row(ref, j):
        return jnp.broadcast_to(ref[pl.ds(j, 1), :], (GROUP, LANES))

    def window(j):
        begin, stop = row(start_f, j), row(end_f, j)
        return begin, stop, [(t >= begin) & (t <= stop) for t in period]

    load[0].wait()
    load[1].wait()
    start_f[...] = start_v[...].astype(F32)
    end_f[...] = end_v[...].astype(F32)

    load[2].wait()

    @pl.loop(0, chunks)
    def _(j):
        begin, stop, active = window(j)
        parts = [jnp.where(active[g], piece(dual_demand_v, g, j), 0.0) for g in range(groups)]
        tails, total = suffix_rows(parts, sub)
        for g in range(groups):
            put(local_v, g, j, tails[g])
        own_v[0, pl.ds(j, 1), :] = total[0:1, :]

    for k in range(3, 7):
        load[k].wait()
    by_block_production = exact(dual_resource_v[...], coef_production_v[...], ((1,), (1,)))
    by_block_setup = exact(dual_resource_v[...], coef_setup_v[...], ((1,), (1,)))
    stacked = jnp.concatenate(
        [t.astype(F32) for t in halves(by_block_production, 3) + halves(by_block_setup, 3)], axis=0
    ).astype(BF16)
    wide = 4

    @pl.loop(0, chunks // wide)
    def _(i):
        for k in range(wide):
            j = i * wide + k
            ids = jnp.broadcast_to(block_v[pl.ds(j, 1), :], (blocks, LANES))
            hot = ids == lax.broadcasted_iota(jnp.int32, (blocks, LANES), 0)
            onehot_v[:, lanes(j)] = jnp.where(hot, 1.0, 0.0).astype(BF16)
        at = pl.ds(pl.multiple_of(i * wide * LANES, wide * LANES), wide * LANES)
        pulled = jnp.dot(stacked, onehot_v[:, at], preferred_element_type=F32)
        pull_production_v[:, at] = pulled[0:rows] + (
            pulled[rows : 2 * rows] + pulled[2 * rows : 3 * rows]
        )
        pull_setup_v[:, at] = pulled[3 * rows : 4 * rows] + (
            pulled[4 * rows : 5 * rows] + pulled[5 * rows : 6 * rows]
        )

    for k in range(7, 16):
        load[k].wait()

    @pl.loop(0, chunks)
    def _(j):
        begin, stop, active = window(j)
        setup_price = row(cost_setup_v, j)
        late_price = row(penalty_v, j)
        for g in range(groups):
            on = active[g]
            dual_active = jnp.where(on, piece(dual_demand_v, g, j), 0.0)
            link_active = jnp.where(on, piece(dual_link_v, g, j), 0.0)
            primal_step = 1.0 / (2.0 + jnp.maximum(stop - period[g], 0.0))
            dual_step = 1.0 / (2.0 + jnp.maximum(period[g] - begin, 0.0))
            price = (
                piece(cost_production_v, g, j)
                - piece(local_v, g, j)
                + link_active
                + piece(pull_production_v, g, j)
            )
            put(local_v, g, j, piece(production_v, g, j) - primal_step * price)
            put(primal_step_v, g, j, primal_step)
            put(dual_step_v, g, j, dual_step)
            before = piece(setup_v, g, j)
            moved = jnp.clip(
                before - setup_step * (setup_price - big_m * link_active + piece(pull_setup_v, g, j)),
                0.0,
                1.0,
            )
            state = piece(fixing_v, g, j)
            moved = jnp.where(state == 1, 0.0, jnp.where(state == 2, 1.0, moved))
            moved = jnp.where(on, moved, 0.0)
            put(setup_v, g, j, moved)
            setup_bar = jnp.where(on, 2.0 * moved - before, 0.0)
            put(setup_bar_v, g, j, setup_bar)
            put(link_v, g, j, link_active - link_step * big_m * setup_bar)
            before = piece(shortage_v, g, j)
            late = jnp.where(
                on, jnp.maximum(before - short_step * (late_price - dual_active), 0.0), 0.0
            )
            put(shortage_v, g, j, late)
            put(dual_demand_v, g, j, dual_active - dual_step * (2.0 * late - before))

    stores = []

    def store(k, src, dst):
        copy = pltpu.make_async_copy(src, dst, out_sem.at[k])
        copy.start()
        stores.append(copy)

    store(0, setup_v, setup_o)
    store(1, shortage_v, shortage_o)

    pl.semaphore_wait(barrier, greeted)

    sent = []

    def remote(src, dst, send, recv, where):
        return pltpu.make_async_remote_copy(
            src_ref=src, dst_ref=dst, send_sem=send, recv_sem=recv, device_id=where, device_id_type=MESH
        )

    mine = pl.ds(pl.multiple_of(core * half, half), half)
    other = pl.ds(pl.multiple_of((1 - core) * half, half), half)

    def carried(s, later):
        def counts(there, here):
            return there > here if later else there < here

        sibling = place(x, z, 1 - core)
        to_core = remote(own_v.at[s], sibling_v.at[s], core_send.at[s], core_recv.at[s], sibling)
        to_core.start()
        sent.append(to_core)
        to_core.wait_recv()
        along_z_v[s, z] = own_v[s, mine, :] + sibling_v[s, mine, :]
        for d in sorted(range(1, nz), key=lambda d: -min(d, nz - d)):
            copy = remote(
                along_z_v.at[s, z],
                along_z_v.at[s, z],
                z_send.at[s, d],
                z_recv.at[s, z],
                place(x, lax.rem(z + d, nz), core),
            )
            copy.start()
            sent.append(copy)
        for d in range(1, nz):
            there = lax.rem(z + d, nz)
            remote(
                along_z_v.at[s, there],
                along_z_v.at[s, there],
                z_send.at[s, d],
                z_recv.at[s, there],
                place(x, there, core),
            ).wait_recv()
        whole = along_z_v[s, 0]
        partial = jnp.where(counts(0, z), whole, 0.0)
        for k in range(1, nz):
            term = along_z_v[s, k]
            whole = whole + term
            partial = partial + jnp.where(counts(k, z), term, 0.0)
        along_x_v[s, x, mine, :] = whole
        inside_v[s, mine, :] = partial
        for d in sorted(range(1, nx), key=lambda d: -min(d, nx - d)):
            for c in range(CORES):
                copy = remote(
                    along_x_v.at[s, x, mine],
                    along_x_v.at[s, x, mine],
                    x_send.at[s, d, c],
                    x_recv.at[s, x, core],
                    place(lax.rem(x + d, nx), z, c),
                )
                copy.start()
                sent.append(copy)
        to_core = remote(
            inside_v.at[s, mine], inside_v.at[s, mine], inside_send.at[s], inside_recv.at[s], sibling
        )
        to_core.start()
        sent.append(to_core)
        remote(
            inside_v.at[s, other], inside_v.at[s, other], inside_send.at[s], inside_recv.at[s], sibling
        ).wait_recv()
        total = inside_v[s] + jnp.where(counts(1 - core, core), sibling_v[s], 0.0)
        for d in range(1, nx):
            there = lax.rem(x + d, nx)
            for c in range(CORES):
                part = pl.ds(c * half, half)
                remote(
                    along_x_v.at[s, there, part],
                    along_x_v.at[s, there, part],
                    x_send.at[s, d, c],
                    x_recv.at[s, there, c],
                    place(there, z, c),
                ).wait_recv()
            total = total + jnp.where(counts(there, x), along_x_v[s, there], 0.0)
        carry_v[s] = total

    carried(0, True)

    @pl.loop(0, chunks)
    def _(j):
        begin, stop, active = window(j)
        carry = row(carry_v.at[0], j)
        total = jnp.zeros((GROUP, LANES), F32)
        for g in range(groups):
            on = active[g]
            before = piece(production_v, g, j)
            made = jnp.maximum(piece(local_v, g, j) + piece(primal_step_v, g, j) * carry, 0.0)
            made = jnp.where(on, made, 0.0)
            put(production_v, g, j, made)
            bar = jnp.where(on, 2.0 * made - before, 0.0)
            put(prod_bar_v, g, j, bar)
            flow = bar - jnp.where(on, piece(demand_v, g, j), 0.0)
            put(flow_v, g, j, flow)
            total = total + flow
        own_v[1, pl.ds(j, 1), :] = jnp.sum(total, axis=0, keepdims=True)

    store(2, production_v, production_o)

    @pl.loop(0, chunks)
    def _(j):
        begin, stop, active = window(j)
        heads = prefix_rows([piece(flow_v, g, j) for g in range(groups)], sub)
        for g in range(groups):
            put(
                dual_demand_v,
                g,
                j,
                piece(dual_demand_v, g, j) - piece(dual_step_v, g, j) * heads[g],
            )
            link = jnp.maximum(piece(link_v, g, j) + link_step * piece(prod_bar_v, g, j), 0.0)
            put(dual_link_v, g, j, jnp.where(active[g], link, 0.0))

    store(3, dual_link_v, dual_link_o)

    deep = DEPTH * LANES

    def add_blocks(i, total):
        at = pl.ds(pl.multiple_of(i * deep, deep), deep)
        terms = halves(prod_bar_v[:, at], 2) + halves(setup_bar_v[:, at], 2)
        left = jnp.concatenate(terms, axis=0)
        return total + lax.dot_general(
            left, onehot_v[:, at], (((1,), (1,)), ((), ())), preferred_element_type=F32
        )

    by_block = lax.fori_loop(0, items // deep, add_blocks, jnp.zeros((4 * rows, blocks), F32))
    usage_v[y] = exact(
        by_block[0:rows] + by_block[rows : 2 * rows], coef_production_v[...], ((1,), (0,))
    ) + exact(
        by_block[2 * rows : 3 * rows] + by_block[3 * rows : 4 * rows], coef_setup_v[...], ((1,), (0,))
    )
    for d in range(1, ny):
        copy = remote(
            usage_v.at[y], usage_v.at[y], y_send.at[d], y_recv.at[y], place(x, z, core, lax.rem(y + d, ny))
        )
        copy.start()
        sent.append(copy)

    carried(1, False)

    @pl.loop(0, chunks)
    def _(j):
        begin, stop, active = window(j)
        carry = row(carry_v.at[1], j)
        for g in range(groups):
            dual = piece(dual_demand_v, g, j) - piece(dual_step_v, g, j) * carry
            put(dual_demand_v, g, j, jnp.where(active[g], jnp.maximum(dual, 0.0), 0.0))

    store(4, dual_demand_v, dual_demand_o)

    for d in range(1, ny):
        there = lax.rem(y + d, ny)
        remote(
            usage_v.at[there], usage_v.at[there], y_send.at[d], y_recv.at[there], place(x, z, core, there)
        ).wait_recv()
    load[16].wait()
    usage = usage_v[0]
    for k in range(1, ny):
        usage = usage + usage_v[k]
    scale = dual_resource_v.shape[1] / items_total
    dual_resource_v[...] = jnp.maximum(dual_resource_v[...] + scale * (usage - capacity_v[...]), 0.0)
    store(5, dual_resource_v, dual_resource_o)

    for copy in stores:
        copy.wait()
    for copy in sent:
        copy.wait_send()


def shards(ranks, items_total, *args):
    (
        production,
        setup,
        shortage,
        dual_demand,
        dual_link,
        dual_resource,
        cost_production,
        cost_setup,
        penalty,
        demand,
        capacity,
        coef_production,
        coef_setup,
        horizon_start,
        horizon_end,
        fixing,
        block_id,
    ) = args
    nx, nz, ny = ranks
    rows, items = production.shape
    resources = dual_resource.shape[1]
    blocks = coef_production.shape[0]
    chunks = items // LANES
    per_item = (chunks, LANES)
    big, vector, small = (rows, items), (chunks, LANES), (rows, resources)

    def vmem(shape, dtype=F32):
        return pltpu.VMEM(shape, dtype)

    dma = pltpu.SemaphoreType.DMA
    anywhere = pl.BlockSpec(memory_space=pl.ANY)
    scratch = (
        [vmem(big)] * 7
        + [vmem(big, jnp.int32)]
        + [vmem(small)] * 2
        + [vmem((blocks, resources))] * 2
        + [vmem(vector)] * 2
        + [vmem(vector, jnp.int32)] * 3
        + [vmem(vector)] * 2
        + [vmem((blocks, items), BF16)]
        + [vmem(big)] * 9
        + [
            vmem((2,) + vector),
            vmem((2,) + vector),
            vmem((2, nz, chunks // 2, LANES)),
            vmem((2, nx) + vector),
            vmem((2,) + vector),
            vmem((2,) + vector),
            vmem((ny,) + small),
        ]
        + [
            dma((17,)),
            dma((6,)),
            dma((2,)),
            dma((2,)),
            dma((2, nz)),
            dma((2, nz)),
            dma((2, nx, CORES)),
            dma((2, nx, CORES)),
            dma((2,)),
            dma((2,)),
            dma((ny,)),
            dma((ny,)),
        ]
    )
    results = pl.pallas_call(
        functools.partial(kernel, ranks, items_total),
        out_shape=[jax.ShapeDtypeStruct(big, F32)] * 5 + [jax.ShapeDtypeStruct(small, F32)],
        in_specs=[pl.BlockSpec(memory_space=pltpu.HBM)] * 17,
        out_specs=[anywhere] * 6,
        scratch_shapes=scratch,
        compiler_params=pltpu.CompilerParams(
            collective_id=0, has_side_effects=True, vmem_limit_bytes=40 * 1024 * 1024
        ),
        name="lot_step",
    )(
        production,
        setup,
        shortage,
        dual_demand,
        dual_link,
        dual_resource,
        cost_production,
        cost_setup.reshape(per_item),
        penalty.reshape(per_item),
        demand,
        capacity,
        coef_production,
        coef_setup,
        horizon_start.reshape(per_item),
        horizon_end.reshape(per_item),
        fixing,
        block_id.reshape(per_item),
    )
    return tuple(results)


def solution(mesh):
    across, ny = mesh.shape["tm"], mesh.shape["items"]
    nz = 8
    nx = across // (nz * CORES)
    placed = (
        P("tm", "items"),
        P("tm", "items"),
        P("tm", "items"),
        P("tm", "items"),
        P("tm", "items"),
        P("tm", None),
        P("tm", "items"),
        P("items"),
        P("items"),
        P("tm", "items"),
        P("tm", None),
        P(),
        P(),
        P("items"),
        P("items"),
        P("tm", "items"),
        P("items"),
    )

    def step(*args):
        return jax.shard_map(
            functools.partial(shards, (nx, nz, ny), args[0].shape[1]),
            mesh=mesh,
            in_specs=placed,
            out_specs=(P("tm", "items"),) * 5 + (P("tm", None),),
            check_vma=False,
        )(*args)

    return step
```

profile of v0, /device:TPU:1, one launch (start us, length us, event | category | flops | bytes accessed | tf_op | source)
XLA Modules:
  0.0 57.3 jit_solution(3213664317968982368)
XLA Ops:
  0.6 0.0 copy-start
  0.6 1.1 %copy-done = f32[48,4096]{1,0:T(8,128)S(1)} copy-done((f32[48,4096]{1,0:T(8,128)S(1)}, f32[48,4096]{1,0:T(8,128)}, u32[]{:S(2)}) %copy-start) | copy-done | bytes 786456
  1.8 0.0 copy-start.1
  1.8 1.1 %copy-done.1 = f32[48,4096]{1,0:T(8,128)S(1)} copy-done((f32[48,4096]{1,0:T(8,128)S(1)}, f32[48,4096]{1,0:T(8,128)}, u32[]{:S(2)}) %copy-start.1) | copy-done | bytes 786456
  2.9 0.0 copy-start.2
  2.9 1.1 %copy-done.2 = f32[48,4096]{1,0:T(8,128)S(1)} copy-done((f32[48,4096]{1,0:T(8,128)S(1)}, f32[48,4096]{1,0:T(8,128)}, u32[]{:S(2)}) %copy-start.2) | copy-done | bytes 786456
  4.0 0.0 copy-start.3
  4.0 1.1 %copy-done.3 = f32[48,4096]{1,0:T(8,128)S(1)} copy-done((f32[48,4096]{1,0:T(8,128)S(1)}, f32[48,4096]{1,0:T(8,128)}, u32[]{:S(2)}) %copy-start.3) | copy-done | bytes 786456
  5.2 0.0 copy-start.4
  5.2 1.1 %copy-done.4 = f32[48,4096]{1,0:T(8,128)S(1)} copy-done((f32[48,4096]{1,0:T(8,128)S(1)}, f32[48,4096]{1,0:T(8,128)}, u32[]{:S(2)}) %copy-start.4) | copy-done | bytes 786456
  6.3 0.0 copy-start.5
  6.3 1.1 %copy-done.5 = f32[48,4096]{1,0:T(8,128)S(1)} copy-done((f32[48,4096]{1,0:T(8,128)S(1)}, f32[48,4096]{1,0:T(8,128)}, u32[]{:S(2)}) %copy-start.5) | copy-done | bytes 786456
  7.4 0.0 copy-start.6
  7.4 1.1 %copy-done.6 = f32[48,4096]{1,0:T(8,128)S(1)} copy-done((f32[48,4096]{1,0:T(8,128)S(1)}, f32[48,4096]{1,0:T(8,128)}, u32[]{:S(2)}) %copy-start.6) | copy-done | bytes 786456
  8.6 0.0 copy-start.7
  8.6 1.1 %copy-done.7 = s32[48,4096]{1,0:T(8,128)S(1)} copy-done((s32[48,4096]{1,0:T(8,128)S(1)}, s32[48,4096]{1,0:T(8,128)}, u32[]{:S(2)}) %copy-start.7) | copy-done | bytes 786456
  9.7 0.0 copy-start.8
  9.7 0.9 %copy-done.8 = f32[256,128]{1,0:T(8,128)S(1)} copy-done((f32[256,128]{1,0:T(8,128)S(1)}, f32[256,128]{1,0:T(8,128)}, u32[]{:S(2)}) %copy-start.8) | copy-done | bytes 131096
  10.6 0.0 copy-start.9
  10.6 0.9 %copy-done.9 = f32[256,128]{1,0:T(8,128)S(1)} copy-done((f32[256,128]{1,0:T(8,128)S(1)}, f32[256,128]{1,0:T(8,128)}, u32[]{:S(2)}) %copy-start.9) | copy-done | bytes 131096
  11.5 0.0 copy-start.10
  11.5 0.7 %copy-done.10 = f32[48,128]{1,0:T(8,128)S(1)} copy-done((f32[48,128]{1,0:T(8,128)S(1)}, f32[48,128]{1,0:T(8,128)}, u32[]{:S(2)}) %copy-start.10) | copy-done | bytes 24600
  12.3 0.0 copy-start.11
  12.3 0.7 %copy-done.11 = f32[48,128]{1,0:T(8,128)S(1)} copy-done((f32[48,128]{1,0:T(8,128)S(1)}, f32[48,128]{1,0:T(8,128)}, u32[]{:S(2)}) %copy-start.11) | copy-done | bytes 24600
  13.0 0.0 copy-start.12
  13.0 0.7 %copy-done.12 = f32[4096]{0:T(1024)S(1)} copy-done((f32[4096]{0:T(1024)S(1)}, f32[4096]{0:T(1024)}, u32[]{:S(2)}) %copy-start.12) | copy-done | bytes 16408
  13.7 0.0 copy-start.13
  13.7 0.7 %copy-done.13 = f32[4096]{0:T(1024)S(1)} copy-done((f32[4096]{0:T(1024)S(1)}, f32[4096]{0:T(1024)}, u32[]{:S(2)}) %copy-start.13) | copy-done | bytes 16408
  14.4 0.0 copy-start.14
  14.4 0.7 %copy-done.14 = s32[4096]{0:T(1024)S(1)} copy-done((s32[4096]{0:T(1024)S(1)}, s32[4096]{0:T(1024)}, u32[]{:S(2)}) %copy-start.14) | copy-done | bytes 16408
  15.1 0.0 copy-start.15
  15.2 0.7 %copy-done.15 = s32[4096]{0:T(1024)S(1)} copy-done((s32[4096]{0:T(1024)S(1)}, s32[4096]{0:T(1024)}, u32[]{:S(2)}) %copy-start.15) | copy-done | bytes 16408
  15.9 0.0 copy-start.16
  15.9 0.7 %copy-done.16 = s32[4096]{0:T(1024)S(1)} copy-done((s32[4096]{0:T(1024)S(1)}, s32[4096]{0:T(1024)}, u32[]{:S(2)}) %copy-start.16) | copy-done | bytes 16408
  16.6 35.7 %lot_step.1 = (f32[48,4096]{1,0:T(8,128)S(1)}, f32[48,4096]{1,0:T(8,128)S(1)}, f32[48,4096]{1,0:T(8,128)S(1)}, f32[48,4096]{1,0:T(8,128)S(1)}, f32[48,4096]{1,0:T(8,128)S(1)}, /*index=5*/f32[48,128]{1,0:T(8,128)S(1)}) custom-call(f32[48,4096]{1,0:T(8,128)S(1)} %copy-done, f32[48,4096]{1,0:T(8,128)S(1)} %copy-done.1, f32[48,4096]{1,0:T(8,128)S(1)} %copy-done.2, ...), custom_call_target="tpu_custom_call" | custom-call | tf_op jit(solution)/shard_map/lot_step/pallas_call | solution.py:557
  52.2 0.9 %copy.29 = f32[48,4096]{1,0:T(8,128)} copy(f32[48,4096]{1,0:T(8,128)S(1)} %get-tuple-element.12) | data formatting | bytes 1572864
  53.1 0.9 %copy.30 = f32[48,4096]{1,0:T(8,128)} copy(f32[48,4096]{1,0:T(8,128)S(1)} %get-tuple-element.13) | data formatting | bytes 1572864
  54.0 0.9 %copy.31 = f32[48,4096]{1,0:T(8,128)} copy(f32[48,4096]{1,0:T(8,128)S(1)} %get-tuple-element.14) | data formatting | bytes 1572864
  54.9 0.9 %copy.32 = f32[48,4096]{1,0:T(8,128)} copy(f32[48,4096]{1,0:T(8,128)S(1)} %get-tuple-element.15) | data formatting | bytes 1572864
  55.8 0.9 %copy.33 = f32[48,4096]{1,0:T(8,128)} copy(f32[48,4096]{1,0:T(8,128)S(1)} %get-tuple-element.16) | data formatting | bytes 1572864
  56.6 0.6 %copy.34 = f32[48,128]{1,0:T(8,128)} copy(f32[48,128]{1,0:T(8,128)S(1)} %get-tuple-element.17) | data formatting | bytes 49152
Async XLA Ops:
  0.6 1.1 %copy-start = (f32[48,4096]{1,0:T(8,128)S(1)}, f32[48,4096]{1,0:T(8,128)}, u32[]{:S(2)}) copy-start(f32[48,4096]{1,0:T(8,128)} %production_h.1) | copy-start | bytes 2359300
  1.8 1.1 %copy-start.1 = (f32[48,4096]{1,0:T(8,128)S(1)}, f32[48,4096]{1,0:T(8,128)}, u32[]{:S(2)}) copy-start(f32[48,4096]{1,0:T(8,128)} %setup_h.1) | copy-start | bytes 2359300
  2.9 1.1 %copy-start.2 = (f32[48,4096]{1,0:T(8,128)S(1)}, f32[48,4096]{1,0:T(8,128)}, u32[]{:S(2)}) copy-start(f32[48,4096]{1,0:T(8,128)} %shortage_h.1) | copy-start | bytes 2359300
  4.0 1.1 %copy-start.3 = (f32[48,4096]{1,0:T(8,128)S(1)}, f32[48,4096]{1,0:T(8,128)}, u32[]{:S(2)}) copy-start(f32[48,4096]{1,0:T(8,128)} %dual_demand_h.1) | copy-start | bytes 2359300
  5.2 1.1 %copy-start.4 = (f32[48,4096]{1,0:T(8,128)S(1)}, f32[48,4096]{1,0:T(8,128)}, u32[]{:S(2)}) copy-start(f32[48,4096]{1,0:T(8,128)} %dual_link_h.1) | copy-start | bytes 2359300
  6.3 1.1 %copy-start.5 = (f32[48,4096]{1,0:T(8,128)S(1)}, f32[48,4096]{1,0:T(8,128)}, u32[]{:S(2)}) copy-start(f32[48,4096]{1,0:T(8,128)} %cost_production_h.1) | copy-start | bytes 2359300
  7.4 1.1 %copy-start.6 = (f32[48,4096]{1,0:T(8,128)S(1)}, f32[48,4096]{1,0:T(8,128)}, u32[]{:S(2)}) copy-start(f32[48,4096]{1,0:T(8,128)} %demand_h.1) | copy-start | bytes 2359300
  8.6 1.1 %copy-start.7 = (s32[48,4096]{1,0:T(8,128)S(1)}, s32[48,4096]{1,0:T(8,128)}, u32[]{:S(2)}) copy-start(s32[48,4096]{1,0:T(8,128)} %fixing_h.1) | copy-start | bytes 2359300
  9.7 0.9 %copy-start.8 = (f32[256,128]{1,0:T(8,128)S(1)}, f32[256,128]{1,0:T(8,128)}, u32[]{:S(2)}) copy-start(f32[256,128]{1,0:T(8,128)} %coef_production_h.1) | copy-start | bytes 393220
  10.6 0.9 %copy-start.9 = (f32[256,128]{1,0:T(8,128)S(1)}, f32[256,128]{1,0:T(8,128)}, u32[]{:S(2)}) copy-start(f32[256,128]{1,0:T(8,128)} %coef_setup_h.1) | copy-start | bytes 393220
  11.5 0.7 %copy-start.10 = (f32[48,128]{1,0:T(8,128)S(1)}, f32[48,128]{1,0:T(8,128)}, u32[]{:S(2)}) copy-start(f32[48,128]{1,0:T(8,128)} %dual_resource_h.1) | copy-start | bytes 73732
  12.3 0.7 %copy-start.11 = (f32[48,128]{1,0:T(8,128)S(1)}, f32[48,128]{1,0:T(8,128)}, u32[]{:S(2)}) copy-start(f32[48,128]{1,0:T(8,128)} %capacity_h.1) | copy-start | bytes 73732
  13.0 0.7 %copy-start.12 = (f32[4096]{0:T(1024)S(1)}, f32[4096]{0:T(1024)}, u32[]{:S(2)}) copy-start(f32[4096]{0:T(1024)} %param.24) | copy-start | bytes 49156
  13.7 0.7 %copy-start.13 = (f32[4096]{0:T(1024)S(1)}, f32[4096]{0:T(1024)}, u32[]{:S(2)}) copy-start(f32[4096]{0:T(1024)} %param.25) | copy-start | bytes 49156
  14.4 0.7 %copy-start.14 = (s32[4096]{0:T(1024)S(1)}, s32[4096]{0:T(1024)}, u32[]{:S(2)}) copy-start(s32[4096]{0:T(1024)} %param.30) | copy-start | bytes 49156
  15.1 0.7 %copy-start.15 = (s32[4096]{0:T(1024)S(1)}, s32[4096]{0:T(1024)}, u32[]{:S(2)}) copy-start(s32[4096]{0:T(1024)} %param.31) | copy-start | bytes 49156
  15.9 0.7 %copy-start.16 = (s32[4096]{0:T(1024)S(1)}, s32[4096]{0:T(1024)}, u32[]{:S(2)}) copy-start(s32[4096]{0:T(1024)} %param.33) | copy-start | bytes 49156
where the time goes:
time: 58.1 us; the launch traced here: 57.3 us
  Pallas kernels  35.7 us (61%)
  local copies, waits for them, and re-layouts  20.9 us (36%)
  between operations  0.68 us (1%)
    pallas_call x1, Pallas kernels, shards(): pl.pallas_call(functools.partial(kernel, ranks, items_total), out_shape=[...  35.7 us
    unnamed x40, local copies, waits for them, and re-layouts  20.9 us

commit v1 on v0

--- a/solution.py
+++ b/solution.py
@@ -84,21 +84,17 @@
     end_h,
     fixing_h,
     block_h,
-    production_o,
-    setup_o,
-    shortage_o,
-    dual_demand_o,
-    dual_link_o,
-    dual_resource_o,
     production_v,
     setup_v,
     shortage_v,
     dual_demand_v,
     dual_link_v,
+    dual_resource_v,
+    dual_step_v,
+    window_v,
     cost_production_v,
     demand_v,
     fixing_v,
-    dual_resource_v,
     capacity_v,
     coef_production_v,
     coef_setup_v,
@@ -107,14 +103,11 @@
     start_v,
     end_v,
     block_v,
-    start_f,
-    end_f,
     onehot_v,
     pull_production_v,
     pull_setup_v,
     local_v,
     primal_step_v,
-    dual_step_v,
     setup_bar_v,
     prod_bar_v,
     link_v,
@@ -124,10 +117,9 @@
     along_z_v,
     along_x_v,
     inside_v,
-    carry_v,
+    first_carry_v,
     usage_v,
     in_sem,
-    out_sem,
     core_send,
     core_recv,
     z_send,
@@ -154,28 +146,35 @@
     def place(px, pz, pc, py=None):
         return ((px * nz + pz) * CORES + pc, y if py is None else py)
 
-    loads = [
-        (start_h, start_v),
-        (end_h, end_v),
-        (dual_demand_h, dual_demand_v),
-        (block_h, block_v),
-        (dual_resource_h, dual_resource_v),
-        (coef_production_h, coef_production_v),
-        (coef_setup_h, coef_setup_v),
-        (cost_setup_h, cost_setup_v),
-        (penalty_h, penalty_v),
-        (dual_link_h, dual_link_v),
-        (setup_h, setup_v),
-        (fixing_h, fixing_v),
-        (shortage_h, shortage_v),
-        (production_h, production_v),
-        (cost_production_h, cost_production_v),
-        (demand_h, demand_v),
-        (capacity_h, capacity_v),
-    ]
-    load = [pltpu.make_async_copy(src, dst, in_sem.at[k]) for k, (src, dst) in enumerate(loads)]
-    for copy in load:
+    loads = {
+        "start": (start_h, start_v),
+        "end": (end_h, end_v),
+        "dual_demand": (dual_demand_h, dual_demand_v),
+        "block": (block_h, block_v),
+        "dual_resource": (dual_resource_h, dual_resource_v),
+        "coef_production": (coef_production_h, coef_production_v),
+        "coef_setup": (coef_setup_h, coef_setup_v),
+        "cost_setup": (cost_setup_h, cost_setup_v),
+        "penalty": (penalty_h, penalty_v),
+        "dual_link": (dual_link_h, dual_link_v),
+        "setup": (setup_h, setup_v),
+        "fixing": (fixing_h, fixing_v),
+        "shortage": (shortage_h, shortage_v),
+        "production": (production_h, production_v),
+        "cost_production": (cost_production_h, cost_production_v),
+        "demand": (demand_h, demand_v),
+        "capacity": (capacity_h, capacity_v),
+    }
+    load = {
+        name: pltpu.make_async_copy(src, dst, in_sem.at[k])
+        for k, (name, (src, dst)) in enumerate(loads.items())
+    }
+    for copy in load.values():
         copy.start()
+
+    def arrived(*names):
+        for name in names:
+            load[name].wait()
 
     barrier = pltpu.get_barrier_semaphore()
     greeted = 0
@@ -215,15 +214,14 @@
         return jnp.broadcast_to(ref[pl.ds(j, 1), :], (GROUP, LANES))
 
     def window(j):
-        begin, stop = row(start_f, j), row(end_f, j)
+        begin, stop = row(window_v.at[0], j), row(window_v.at[1], j)
         return begin, stop, [(t >= begin) & (t <= stop) for t in period]
 
-    load[0].wait()
-    load[1].wait()
-    start_f[...] = start_v[...].astype(F32)
-    end_f[...] = end_v[...].astype(F32)
-
-    load[2].wait()
+    arrived("start", "end")
+    window_v[0] = start_v[...].astype(F32)
+    window_v[1] = end_v[...].astype(F32)
+
+    arrived("dual_demand")
 
     @pl.loop(0, chunks)
     def _(j):
@@ -234,8 +232,7 @@
             put(local_v, g, j, tails[g])
         own_v[0, pl.ds(j, 1), :] = total[0:1, :]
 
-    for k in range(3, 7):
-        load[k].wait()
+    arrived("block", "dual_resource", "coef_production", "coef_setup")
     by_block_production = exact(dual_resource_v[...], coef_production_v[...], ((1,), (1,)))
     by_block_setup = exact(dual_resource_v[...], coef_setup_v[...], ((1,), (1,)))
     stacked = jnp.concatenate(
@@ -259,59 +256,6 @@
             pulled[4 * rows : 5 * rows] + pulled[5 * rows : 6 * rows]
         )
 
-    for k in range(7, 16):
-        load[k].wait()
-
-    @pl.loop(0, chunks)
-    def _(j):
-        begin, stop, active = window(j)
-        setup_price = row(cost_setup_v, j)
-        late_price = row(penalty_v, j)
-        for g in range(groups):
-            on = active[g]
-            dual_active = jnp.where(on, piece(dual_demand_v, g, j), 0.0)
-            link_active = jnp.where(on, piece(dual_link_v, g, j), 0.0)
-            primal_step = 1.0 / (2.0 + jnp.maximum(stop - period[g], 0.0))
-            dual_step = 1.0 / (2.0 + jnp.maximum(period[g] - begin, 0.0))
-            price = (
-                piece(cost_production_v, g, j)
-                - piece(local_v, g, j)
-                + link_active
-                + piece(pull_production_v, g, j)
-            )
-            put(local_v, g, j, piece(production_v, g, j) - primal_step * price)
-            put(primal_step_v, g, j, primal_step)
-            put(dual_step_v, g, j, dual_step)
-            before = piece(setup_v, g, j)
-            moved = jnp.clip(
-                before - setup_step * (setup_price - big_m * link_active + piece(pull_setup_v, g, j)),
-                0.0,
-                1.0,
-            )
-            state = piece(fixing_v, g, j)
-            moved = jnp.where(state == 1, 0.0, jnp.where(state == 2, 1.0, moved))
-            moved = jnp.where(on, moved, 0.0)
-            put(setup_v, g, j, moved)
-            setup_bar = jnp.where(on, 2.0 * moved - before, 0.0)
-            put(setup_bar_v, g, j, setup_bar)
-            put(link_v, g, j, link_active - link_step * big_m * setup_bar)
-            before = piece(shortage_v, g, j)
-            late = jnp.where(
-                on, jnp.maximum(before - short_step * (late_price - dual_active), 0.0), 0.0
-            )
-            put(shortage_v, g, j, late)
-            put(dual_demand_v, g, j, dual_active - dual_step * (2.0 * late - before))
-
-    stores = []
-
-    def store(k, src, dst):
-        copy = pltpu.make_async_copy(src, dst, out_sem.at[k])
-        copy.start()
-        stores.append(copy)
-
-    store(0, setup_v, setup_o)
-    store(1, shortage_v, shortage_o)
-
     pl.semaphore_wait(barrier, greeted)
 
     sent = []
@@ -324,15 +268,24 @@
     mine = pl.ds(pl.multiple_of(core * half, half), half)
     other = pl.ds(pl.multiple_of((1 - core) * half, half), half)
 
-    def carried(s, later):
+    sibling = place(x, z, 1 - core)
+
+    def halfway(s, h):
+        part = pl.ds(pl.multiple_of(h * half, half), half)
+        return remote(
+            own_v.at[s, part], sibling_v.at[s, part], core_send.at[s, h], core_recv.at[s, h], sibling
+        )
+
+    def hand_over(s, h):
+        copy = halfway(s, h)
+        copy.start()
+        sent.append(copy)
+
+    def carried(s, later, during_z, during_x):
         def counts(there, here):
             return there > here if later else there < here
 
-        sibling = place(x, z, 1 - core)
-        to_core = remote(own_v.at[s], sibling_v.at[s], core_send.at[s], core_recv.at[s], sibling)
-        to_core.start()
-        sent.append(to_core)
-        to_core.wait_recv()
+        halfway(s, core).wait_recv()
         along_z_v[s, z] = own_v[s, mine, :] + sibling_v[s, mine, :]
         for d in sorted(range(1, nz), key=lambda d: -min(d, nz - d)):
             copy = remote(
@@ -344,6 +297,7 @@
             )
             copy.start()
             sent.append(copy)
+        during_z()
         for d in range(1, nz):
             there = lax.rem(z + d, nz)
             remote(
@@ -377,6 +331,8 @@
         )
         to_core.start()
         sent.append(to_core)
+        during_x()
+        halfway(s, 1 - core).wait_recv()
         remote(
             inside_v.at[s, other], inside_v.at[s, other], inside_send.at[s], inside_recv.at[s], sibling
         ).wait_recv()
@@ -393,14 +349,69 @@
                     place(there, z, c),
                 ).wait_recv()
             total = total + jnp.where(counts(there, x), along_x_v[s, there], 0.0)
-        carry_v[s] = total
-
-    carried(0, True)
-
-    @pl.loop(0, chunks)
-    def _(j):
+        return total
+
+    def own_part():
+        arrived(
+            "cost_setup",
+            "penalty",
+            "dual_link",
+            "setup",
+            "fixing",
+            "shortage",
+            "production",
+            "cost_production",
+        )
+
+        @pl.loop(0, chunks)
+        def _(j):
+            begin, stop, active = window(j)
+            setup_price = row(cost_setup_v, j)
+            late_price = row(penalty_v, j)
+            for g in range(groups):
+                on = active[g]
+                dual_active = jnp.where(on, piece(dual_demand_v, g, j), 0.0)
+                link_active = jnp.where(on, piece(dual_link_v, g, j), 0.0)
+                primal_step = 1.0 / (2.0 + jnp.maximum(stop - period[g], 0.0))
+                dual_step = 1.0 / (2.0 + jnp.maximum(period[g] - begin, 0.0))
+                price = (
+                    piece(cost_production_v, g, j)
+                    - piece(local_v, g, j)
+                    + link_active
+                    + piece(pull_production_v, g, j)
+                )
+                put(local_v, g, j, piece(production_v, g, j) - primal_step * price)
+                put(primal_step_v, g, j, primal_step)
+                put(dual_step_v, g, j, dual_step)
+                before = piece(setup_v, g, j)
+                moved = jnp.clip(
+                    before - setup_step * (setup_price - big_m * link_active + piece(pull_setup_v, g, j)),
+                    0.0,
+                    1.0,
+                )
+                state = piece(fixing_v, g, j)
+                moved = jnp.where(state == 1, 0.0, jnp.where(state == 2, 1.0, moved))
+                moved = jnp.where(on, moved, 0.0)
+                put(setup_v, g, j, moved)
+                setup_bar = jnp.where(on, 2.0 * moved - before, 0.0)
+                put(setup_bar_v, g, j, setup_bar)
+                put(link_v, g, j, link_active - link_step * big_m * setup_bar)
+                before = piece(shortage_v, g, j)
+                late = jnp.where(
+                    on, jnp.maximum(before - short_step * (late_price - dual_active), 0.0), 0.0
+                )
+                put(shortage_v, g, j, late)
+                put(dual_demand_v, g, j, dual_active - dual_step * (2.0 * late - before))
+
+    hand_over(0, 1 - core)
+    hand_over(0, core)
+    first_carry_v[...] = carried(0, True, own_part, lambda: None)
+
+    arrived("demand")
+
+    def net_production(j):
         begin, stop, active = window(j)
-        carry = row(carry_v.at[0], j)
+        carry = row(first_carry_v, j)
         total = jnp.zeros((GROUP, LANES), F32)
         for g in range(groups):
             on = active[g]
@@ -415,76 +426,116 @@
             total = total + flow
         own_v[1, pl.ds(j, 1), :] = jnp.sum(total, axis=0, keepdims=True)
 
-    store(2, production_v, production_o)
-
-    @pl.loop(0, chunks)
-    def _(j):
-        begin, stop, active = window(j)
-        heads = prefix_rows([piece(flow_v, g, j) for g in range(groups)], sub)
-        for g in range(groups):
-            put(
-                dual_demand_v,
-                g,
-                j,
-                piece(dual_demand_v, g, j) - piece(dual_step_v, g, j) * heads[g],
+    for h in (1 - core, core):
+        pl.loop(h * half, (h + 1) * half)(net_production)
+        hand_over(1, h)
+
+    def dual_part():
+        @pl.loop(0, chunks)
+        def _(j):
+            begin, stop, active = window(j)
+            heads = prefix_rows([piece(flow_v, g, j) for g in range(groups)], sub)
+            for g in range(groups):
+                put(
+                    dual_demand_v,
+                    g,
+                    j,
+                    piece(dual_demand_v, g, j) - piece(dual_step_v, g, j) * heads[g],
+                )
+                link = jnp.maximum(piece(link_v, g, j) + link_step * piece(prod_bar_v, g, j), 0.0)
+                put(dual_link_v, g, j, jnp.where(active[g], link, 0.0))
+
+        deep = DEPTH * LANES
+
+        def add_blocks(i, total):
+            at = pl.ds(pl.multiple_of(i * deep, deep), deep)
+            terms = halves(prod_bar_v[:, at], 2) + halves(setup_bar_v[:, at], 2)
+            left = jnp.concatenate(terms, axis=0)
+            return total + lax.dot_general(
+                left, onehot_v[:, at], (((1,), (1,)), ((), ())), preferred_element_type=F32
             )
-            link = jnp.maximum(piece(link_v, g, j) + link_step * piece(prod_bar_v, g, j), 0.0)
-            put(dual_link_v, g, j, jnp.where(active[g], link, 0.0))
-
-    store(3, dual_link_v, dual_link_o)
-
-    deep = DEPTH * LANES
-
-    def add_blocks(i, total):
-        at = pl.ds(pl.multiple_of(i * deep, deep), deep)
-        terms = halves(prod_bar_v[:, at], 2) + halves(setup_bar_v[:, at], 2)
-        left = jnp.concatenate(terms, axis=0)
-        return total + lax.dot_general(
-            left, onehot_v[:, at], (((1,), (1,)), ((), ())), preferred_element_type=F32
-        )
-
-    by_block = lax.fori_loop(0, items // deep, add_blocks, jnp.zeros((4 * rows, blocks), F32))
-    usage_v[y] = exact(
-        by_block[0:rows] + by_block[rows : 2 * rows], coef_production_v[...], ((1,), (0,))
-    ) + exact(
-        by_block[2 * rows : 3 * rows] + by_block[3 * rows : 4 * rows], coef_setup_v[...], ((1,), (0,))
-    )
-    for d in range(1, ny):
-        copy = remote(
-            usage_v.at[y], usage_v.at[y], y_send.at[d], y_recv.at[y], place(x, z, core, lax.rem(y + d, ny))
-        )
-        copy.start()
-        sent.append(copy)
-
-    carried(1, False)
-
-    @pl.loop(0, chunks)
-    def _(j):
-        begin, stop, active = window(j)
-        carry = row(carry_v.at[1], j)
-        for g in range(groups):
-            dual = piece(dual_demand_v, g, j) - piece(dual_step_v, g, j) * carry
-            put(dual_demand_v, g, j, jnp.where(active[g], jnp.maximum(dual, 0.0), 0.0))
-
-    store(4, dual_demand_v, dual_demand_o)
-
-    for d in range(1, ny):
-        there = lax.rem(y + d, ny)
-        remote(
-            usage_v.at[there], usage_v.at[there], y_send.at[d], y_recv.at[there], place(x, z, core, there)
-        ).wait_recv()
-    load[16].wait()
-    usage = usage_v[0]
-    for k in range(1, ny):
-        usage = usage + usage_v[k]
-    scale = dual_resource_v.shape[1] / items_total
-    dual_resource_v[...] = jnp.maximum(dual_resource_v[...] + scale * (usage - capacity_v[...]), 0.0)
-    store(5, dual_resource_v, dual_resource_o)
-
-    for copy in stores:
-        copy.wait()
+
+        by_block = lax.fori_loop(0, items // deep, add_blocks, jnp.zeros((4 * rows, blocks), F32))
+        usage_v[y] = exact(
+            by_block[0:rows] + by_block[rows : 2 * rows], coef_production_v[...], ((1,), (0,))
+        ) + exact(
+            by_block[2 * rows : 3 * rows] + by_block[3 * rows : 4 * rows], coef_setup_v[...], ((1,), (0,))
+        )
+        for d in range(1, ny):
+            copy = remote(
+                usage_v.at[y], usage_v.at[y], y_send.at[d], y_recv.at[y], place(x, z, core, lax.rem(y + d, ny))
+            )
+            copy.start()
+            sent.append(copy)
+
+    def resource_part():
+        for d in range(1, ny):
+            there = lax.rem(y + d, ny)
+            remote(
+                usage_v.at[there], usage_v.at[there], y_send.at[d], y_recv.at[there], place(x, z, core, there)
+            ).wait_recv()
+        arrived("capacity")
+        usage = usage_v[0]
+        for k in range(1, ny):
+            usage = usage + usage_v[k]
+        scale = dual_resource_v.shape[1] / items_total
+        dual_resource_v[...] = jnp.maximum(dual_resource_v[...] + scale * (usage - capacity_v[...]), 0.0)
+
+    window_v[2] = carried(1, False, dual_part, resource_part)
+
     for copy in sent:
         copy.wait_send()
+
+
+def finish(
+    production_v,
+    setup_v,
+    shortage_v,
+    dual_demand_v,
+    dual_link_v,
+    dual_resource_v,
+    dual_step_v,
+    window_v,
+    production_o,
+    setup_o,
+    shortage_o,
+    dual_demand_o,
+    dual_link_o,
+    dual_resource_o,
+    result_v,
+    out_sem,
+):
+    pairs = [
+        (production_v, production_o),
+        (setup_v, setup_o),
+        (shortage_v, shortage_o),
+        (dual_link_v, dual_link_o),
+        (dual_resource_v, dual_resource_o),
+    ]
+    copies = [pltpu.make_async_copy(src, dst, out_sem.at[k]) for k, (src, dst) in enumerate(pairs)]
+    for copy in copies:
+        copy.start()
+    rows, items = result_v.shape
+    first = (lax.axis_index("tm") * rows).astype(F32)
+    sub = lax.broadcasted_iota(jnp.int32, (GROUP, LANES), 0).astype(F32)
+
+    @pl.loop(0, items // LANES)
+    def _(j):
+        at = pl.ds(pl.multiple_of(j * LANES, LANES), LANES)
+        begin, stop, carry = [
+            jnp.broadcast_to(window_v[k, pl.ds(j, 1), :], (GROUP, LANES)) for k in range(3)
+        ]
+        for g in range(rows // GROUP):
+            t = sub + (first + float(g * GROUP))
+            band = slice(g * GROUP, (g + 1) * GROUP)
+            dual = jnp.maximum(dual_demand_v[band, at] - dual_step_v[band, at] * carry, 0.0)
+            result_v[band, at] = jnp.where((t >= begin) & (t <= stop), dual, 0.0)
+
+    last = pltpu.make_async_copy(result_v, dual_demand_o, out_sem.at[len(pairs)])
+    last.start()
+    for copy in copies:
+        copy.wait()
+    last.wait()
 
 
 def shards(ranks, items_total, *args):
@@ -521,29 +572,27 @@
     dma = pltpu.SemaphoreType.DMA
     anywhere = pl.BlockSpec(memory_space=pl.ANY)
     scratch = (
-        [vmem(big)] * 7
+        [vmem(big)] * 2
         + [vmem(big, jnp.int32)]
-        + [vmem(small)] * 2
+        + [vmem(small)]
         + [vmem((blocks, resources))] * 2
         + [vmem(vector)] * 2
         + [vmem(vector, jnp.int32)] * 3
-        + [vmem(vector)] * 2
         + [vmem((blocks, items), BF16)]
-        + [vmem(big)] * 9
+        + [vmem(big)] * 8
         + [
             vmem((2,) + vector),
             vmem((2,) + vector),
             vmem((2, nz, chunks // 2, LANES)),
             vmem((2, nx) + vector),
             vmem((2,) + vector),
-            vmem((2,) + vector),
+            vmem(vector),
             vmem((ny,) + small),
         ]
         + [
             dma((17,)),
-            dma((6,)),
-            dma((2,)),
-            dma((2,)),
+            dma((2, CORES)),
+            dma((2, CORES)),
             dma((2, nz)),
             dma((2, nz)),
             dma((2, nx, CORES)),
@@ -554,17 +603,7 @@
             dma((ny,)),
         ]
     )
-    results = pl.pallas_call(
-        functools.partial(kernel, ranks, items_total),
-        out_shape=[jax.ShapeDtypeStruct(big, F32)] * 5 + [jax.ShapeDtypeStruct(small, F32)],
-        in_specs=[pl.BlockSpec(memory_space=pltpu.HBM)] * 17,
-        out_specs=[anywhere] * 6,
-        scratch_shapes=scratch,
-        compiler_params=pltpu.CompilerParams(
-            collective_id=0, has_side_effects=True, vmem_limit_bytes=40 * 1024 * 1024
-        ),
-        name="lot_step",
-    )(
+    operands = [
         production,
         setup,
         shortage,
@@ -582,7 +621,30 @@
         horizon_end.reshape(per_item),
         fixing,
         block_id.reshape(per_item),
-    )
+    ]
+    operands = [pltpu.with_memory_space_constraint(a, pltpu.HBM) for a in operands]
+    held = pl.BlockSpec(memory_space=pltpu.VMEM)
+    between = [big] * 5 + [small, big, (3,) + vector]
+    parts = pl.pallas_call(
+        functools.partial(kernel, ranks, items_total),
+        out_shape=[pltpu.VMEM(shape, F32) for shape in between],
+        in_specs=[anywhere] * 17,
+        out_specs=[held] * len(between),
+        scratch_shapes=scratch,
+        compiler_params=pltpu.CompilerParams(
+            collective_id=0, has_side_effects=True, vmem_limit_bytes=40 * 1024 * 1024
+        ),
+        name="lot_step",
+    )(*operands)
+    results = pl.pallas_call(
+        finish,
+        out_shape=[jax.ShapeDtypeStruct(big, F32)] * 5 + [jax.ShapeDtypeStruct(small, F32)],
+        in_specs=[held] * len(between),
+        out_specs=[anywhere] * 6,
+        scratch_shapes=[vmem(big), dma((6,))],
+        compiler_params=pltpu.CompilerParams(vmem_limit_bytes=8 * 1024 * 1024),
+        name="finish",
+    )(*parts)
     return tuple(results)
 
 

time: 58.1 us -> 33.1 us (0.57); the launches traced: 57.3 us -> 32.9 us
  local copies, waits for them, and re-layouts: 20.9 us -> 0 us
  Pallas kernels: 35.7 us -> 32.3 us
    unnamed x40 -> x0, local copies, waits for them, and re-layouts: 20.9 us -> none
    pallas_call x1, Pallas kernels: 35.7 us -> 30.3 us  [shards(): pl.pallas_call(functools.partial(kernel, ranks, items_total), out_shape=[...]
    pallas_call x0 -> x1, Pallas kernels: none -> 1.98 us  [shards(): pl.pallas_call(finish, out_shape=[jax.ShapeDtypeStruct(big, F32)] * 5 + [...]
where the time goes in v1:
time: 33.1 us; the launch traced here: 32.9 us
  Pallas kernels  32.3 us (98%)
  between operations  0.65 us (2%)
    pallas_call x1, Pallas kernels, shards(): pl.pallas_call(functools.partial(kernel, ranks, items_total), out_shape=[...  30.3 us
    pallas_call x1, Pallas kernels, shards(): pl.pallas_call(finish, out_shape=[jax.ShapeDtypeStruct(big, F32)] * 5 + [...  1.98 us

profile of v1, /device:TPU:1, one launch (start us, length us, event | category | flops | bytes accessed | tf_op | source)
XLA Modules:
  0.0 32.9 jit_solution(14237149368718168263)
XLA Ops:
  0.6 30.3 %lot_step.1 = (f32[48,4096]{1,0:T(8,128)S(1)}, f32[48,4096]{1,0:T(8,128)S(1)}, f32[48,4096]{1,0:T(8,128)S(1)}, f32[48,4096]{1,0:T(8,128)S(1)}, f32[48,4096]{1,0:...) custom-call(f32[48,4096]{1,0:T(8,128)} %production_h.1, ...), custom_call_target="tpu_custom_call" | custom-call | tf_op jit(solution)/shard_map/lot_step/pallas_call | solution.py:628
  30.9 2.0 %finish.1 = (f32[48,4096]{1,0:T(8,128)}, f32[48,4096]{1,0:T(8,128)}, f32[48,4096]{1,0:T(8,128)}, f32[48,4096]{1,0:T(8,128)}, f32[48,4096]{1,0:T(8,128)}, /*index=5*/f32[48,128]{1,0:T(8,128)}) custom-call(f32[48,4096]{1,0:T(8,128)S(1)} %get-tuple-element.14.production_v, f32[48,4096]{1,0:T(8,128)S(1)} %get-tuple-element.15.setup_v, ...), custom_call_target="tpu_custom_call" | custom-call | tf_op jit(solution)/shard_map/finish/pallas_call | solution.py:639

commit v2 on v1

--- a/solution.py
+++ b/solution.py
@@ -20,6 +20,8 @@
 GROUP = 8
 CORES = 2
 DEPTH = 8
+UNROLL = 4
+PIECES = 4
 
 
 def suffix_rows(groups, sub):
@@ -56,6 +58,10 @@
         if k + 1 < count:
             value = value - term.astype(F32)
     return terms
+
+
+def far_first(count):
+    return sorted(range(1, count), key=lambda d: -min(d, count - d))
 
 
 def exact(left, right, contract):
@@ -111,13 +117,12 @@
     setup_bar_v,
     prod_bar_v,
     link_v,
-    flow_v,
     own_v,
     sibling_v,
     along_z_v,
     along_x_v,
     inside_v,
-    first_carry_v,
+    carry_v,
     usage_v,
     in_sem,
     core_send,
@@ -145,6 +150,27 @@
 
     def place(px, pz, pc, py=None):
         return ((px * nz + pz) * CORES + pc, y if py is None else py)
+
+    barrier = pltpu.get_barrier_semaphore()
+    greeted = 0
+    for d in far_first(nz):
+        pl.semaphore_signal(
+            barrier, inc=1, device_id=place(x, lax.rem(z + d, nz), core), device_id_type=MESH
+        )
+        greeted += 1
+    for d in far_first(nx):
+        for c in range(CORES):
+            pl.semaphore_signal(
+                barrier, inc=1, device_id=place(lax.rem(x + d, nx), z, c), device_id_type=MESH
+            )
+            greeted += 1
+    for d in range(1, ny):
+        pl.semaphore_signal(
+            barrier, inc=1, device_id=place(x, z, core, lax.rem(y + d, ny)), device_id_type=MESH
+        )
+        greeted += 1
+    pl.semaphore_signal(barrier, inc=1, device_id=place(x, z, 1 - core), device_id_type=MESH)
+    greeted += 1
 
     loads = {
         "start": (start_h, start_v),
@@ -176,27 +202,6 @@
         for name in names:
             load[name].wait()
 
-    barrier = pltpu.get_barrier_semaphore()
-    greeted = 0
-    for d in range(1, nz):
-        pl.semaphore_signal(
-            barrier, inc=1, device_id=place(x, lax.rem(z + d, nz), core), device_id_type=MESH
-        )
-        greeted += 1
-    for d in range(1, nx):
-        for c in range(CORES):
-            pl.semaphore_signal(
-                barrier, inc=1, device_id=place(lax.rem(x + d, nx), z, c), device_id_type=MESH
-            )
-            greeted += 1
-    for d in range(1, ny):
-        pl.semaphore_signal(
-            barrier, inc=1, device_id=place(x, z, core, lax.rem(y + d, ny)), device_id_type=MESH
-        )
-        greeted += 1
-    pl.semaphore_signal(barrier, inc=1, device_id=place(x, z, 1 - core), device_id_type=MESH)
-    greeted += 1
-
     sub = lax.broadcasted_iota(jnp.int32, (GROUP, LANES), 0)
     first = (tm * rows).astype(F32)
     period = [sub.astype(F32) + (first + float(g * GROUP)) for g in range(groups)]
@@ -232,30 +237,6 @@
             put(local_v, g, j, tails[g])
         own_v[0, pl.ds(j, 1), :] = total[0:1, :]
 
-    arrived("block", "dual_resource", "coef_production", "coef_setup")
-    by_block_production = exact(dual_resource_v[...], coef_production_v[...], ((1,), (1,)))
-    by_block_setup = exact(dual_resource_v[...], coef_setup_v[...], ((1,), (1,)))
-    stacked = jnp.concatenate(
-        [t.astype(F32) for t in halves(by_block_production, 3) + halves(by_block_setup, 3)], axis=0
-    ).astype(BF16)
-    wide = 4
-
-    @pl.loop(0, chunks // wide)
-    def _(i):
-        for k in range(wide):
-            j = i * wide + k
-            ids = jnp.broadcast_to(block_v[pl.ds(j, 1), :], (blocks, LANES))
-            hot = ids == lax.broadcasted_iota(jnp.int32, (blocks, LANES), 0)
-            onehot_v[:, lanes(j)] = jnp.where(hot, 1.0, 0.0).astype(BF16)
-        at = pl.ds(pl.multiple_of(i * wide * LANES, wide * LANES), wide * LANES)
-        pulled = jnp.dot(stacked, onehot_v[:, at], preferred_element_type=F32)
-        pull_production_v[:, at] = pulled[0:rows] + (
-            pulled[rows : 2 * rows] + pulled[2 * rows : 3 * rows]
-        )
-        pull_setup_v[:, at] = pulled[3 * rows : 4 * rows] + (
-            pulled[4 * rows : 5 * rows] + pulled[5 * rows : 6 * rows]
-        )
-
     pl.semaphore_wait(barrier, greeted)
 
     sent = []
@@ -281,13 +262,22 @@
         copy.start()
         sent.append(copy)
 
+    def across(s, d, c):
+        return remote(
+            along_x_v.at[s, x, mine],
+            along_x_v.at[s, x, mine],
+            x_send.at[s, d, c],
+            x_recv.at[s, x, core],
+            place(lax.rem(x + d, nx), z, c),
+        )
+
     def carried(s, later, during_z, during_x):
         def counts(there, here):
             return there > here if later else there < here
 
         halfway(s, core).wait_recv()
         along_z_v[s, z] = own_v[s, mine, :] + sibling_v[s, mine, :]
-        for d in sorted(range(1, nz), key=lambda d: -min(d, nz - d)):
+        for d in far_first(nz):
             copy = remote(
                 along_z_v.at[s, z],
                 along_z_v.at[s, z],
@@ -315,17 +305,14 @@
             partial = partial + jnp.where(counts(k, z), term, 0.0)
         along_x_v[s, x, mine, :] = whole
         inside_v[s, mine, :] = partial
-        for d in sorted(range(1, nx), key=lambda d: -min(d, nx - d)):
-            for c in range(CORES):
-                copy = remote(
-                    along_x_v.at[s, x, mine],
-                    along_x_v.at[s, x, mine],
-                    x_send.at[s, d, c],
-                    x_recv.at[s, x, core],
-                    place(lax.rem(x + d, nx), z, c),
-                )
-                copy.start()
-                sent.append(copy)
+        for d in far_first(nx):
+            there = lax.rem(x + d, nx)
+
+            @pl.when(counts(x, there))
+            def _():
+                for c in range(CORES):
+                    across(s, d, c).start()
+
         to_core = remote(
             inside_v.at[s, mine], inside_v.at[s, mine], inside_send.at[s], inside_recv.at[s], sibling
         )
@@ -336,20 +323,59 @@
         remote(
             inside_v.at[s, other], inside_v.at[s, other], inside_send.at[s], inside_recv.at[s], sibling
         ).wait_recv()
-        total = inside_v[s] + jnp.where(counts(1 - core, core), sibling_v[s], 0.0)
-        for d in range(1, nx):
+        carry_v[s] = inside_v[s] + jnp.where(counts(1 - core, core), sibling_v[s], 0.0)
+        for d in reversed(far_first(nx)):
             there = lax.rem(x + d, nx)
-            for c in range(CORES):
-                part = pl.ds(c * half, half)
-                remote(
-                    along_x_v.at[s, there, part],
-                    along_x_v.at[s, there, part],
-                    x_send.at[s, d, c],
-                    x_recv.at[s, there, c],
-                    place(there, z, c),
-                ).wait_recv()
-            total = total + jnp.where(counts(there, x), along_x_v[s, there], 0.0)
-        return total
+
+            @pl.when(counts(there, x))
+            def _():
+                for c in range(CORES):
+                    part = pl.ds(c * half, half)
+                    remote(
+                        along_x_v.at[s, there, part],
+                        along_x_v.at[s, there, part],
+                        x_send.at[s, d, c],
+                        x_recv.at[s, there, c],
+                        place(there, z, c),
+                    ).wait_recv()
+                carry_v[s] += along_x_v[s, there]
+
+    def left(s, later):
+        for copy in sent:
+            copy.wait_send()
+        sent.clear()
+        for d in far_first(nx):
+            there = lax.rem(x + d, nx)
+
+            @pl.when(x > there if later else x < there)
+            def _():
+                for c in range(CORES):
+                    across(s, d, c).wait_send()
+
+    def pull():
+        arrived("block", "dual_resource", "coef_production", "coef_setup")
+        by_block_production = exact(dual_resource_v[...], coef_production_v[...], ((1,), (1,)))
+        by_block_setup = exact(dual_resource_v[...], coef_setup_v[...], ((1,), (1,)))
+        stacked = jnp.concatenate(
+            [t.astype(F32) for t in halves(by_block_production, 3) + halves(by_block_setup, 3)], axis=0
+        ).astype(BF16)
+        wide = 4
+
+        @pl.loop(0, chunks // wide)
+        def _(i):
+            for k in range(wide):
+                j = i * wide + k
+                ids = jnp.broadcast_to(block_v[pl.ds(j, 1), :], (blocks, LANES))
+                hot = ids == lax.broadcasted_iota(jnp.int32, (blocks, LANES), 0)
+                onehot_v[:, lanes(j)] = jnp.where(hot, 1.0, 0.0).astype(BF16)
+            at = pl.ds(pl.multiple_of(i * wide * LANES, wide * LANES), wide * LANES)
+            pulled = jnp.dot(stacked, onehot_v[:, at], preferred_element_type=F32)
+            pull_production_v[:, at] = pulled[0:rows] + (
+                pulled[rows : 2 * rows] + pulled[2 * rows : 3 * rows]
+            )
+            pull_setup_v[:, at] = pulled[3 * rows : 4 * rows] + (
+                pulled[4 * rows : 5 * rows] + pulled[5 * rows : 6 * rows]
+            )
 
     def own_part():
         arrived(
@@ -405,13 +431,13 @@
 
     hand_over(0, 1 - core)
     hand_over(0, core)
-    first_carry_v[...] = carried(0, True, own_part, lambda: None)
+    carried(0, True, pull, own_part)
 
     arrived("demand")
 
     def net_production(j):
         begin, stop, active = window(j)
-        carry = row(first_carry_v, j)
+        carry = row(carry_v.at[0], j)
         total = jnp.zeros((GROUP, LANES), F32)
         for g in range(groups):
             on = active[g]
@@ -421,20 +447,27 @@
             put(production_v, g, j, made)
             bar = jnp.where(on, 2.0 * made - before, 0.0)
             put(prod_bar_v, g, j, bar)
-            flow = bar - jnp.where(on, piece(demand_v, g, j), 0.0)
-            put(flow_v, g, j, flow)
-            total = total + flow
+            total = total + (bar - jnp.where(on, piece(demand_v, g, j), 0.0))
         own_v[1, pl.ds(j, 1), :] = jnp.sum(total, axis=0, keepdims=True)
 
     for h in (1 - core, core):
-        pl.loop(h * half, (h + 1) * half)(net_production)
+
+        @pl.loop(0, half // UNROLL)
+        def _(i):
+            for k in range(UNROLL):
+                net_production(h * half + i * UNROLL + k)
+
         hand_over(1, h)
 
     def dual_part():
         @pl.loop(0, chunks)
         def _(j):
             begin, stop, active = window(j)
-            heads = prefix_rows([piece(flow_v, g, j) for g in range(groups)], sub)
+            flow = [
+                piece(prod_bar_v, g, j) - jnp.where(active[g], piece(demand_v, g, j), 0.0)
+                for g in range(groups)
+            ]
+            heads = prefix_rows(flow, sub)
             for g in range(groups):
                 put(
                     dual_demand_v,
@@ -481,10 +514,13 @@
         scale = dual_resource_v.shape[1] / items_total
         dual_resource_v[...] = jnp.maximum(dual_resource_v[...] + scale * (usage - capacity_v[...]), 0.0)
 
-    window_v[2] = carried(1, False, dual_part, resource_part)
-
-    for copy in sent:
-        copy.wait_send()
+    def rest():
+        resource_part()
+        left(0, True)
+
+    carried(1, False, dual_part, rest)
+    window_v[2] = carry_v[1]
+    left(1, False)
 
 
 def finish(
@@ -519,23 +555,30 @@
     first = (lax.axis_index("tm") * rows).astype(F32)
     sub = lax.broadcasted_iota(jnp.int32, (GROUP, LANES), 0).astype(F32)
 
-    @pl.loop(0, items // LANES)
-    def _(j):
-        at = pl.ds(pl.multiple_of(j * LANES, LANES), LANES)
-        begin, stop, carry = [
-            jnp.broadcast_to(window_v[k, pl.ds(j, 1), :], (GROUP, LANES)) for k in range(3)
-        ]
-        for g in range(rows // GROUP):
-            t = sub + (first + float(g * GROUP))
-            band = slice(g * GROUP, (g + 1) * GROUP)
-            dual = jnp.maximum(dual_demand_v[band, at] - dual_step_v[band, at] * carry, 0.0)
-            result_v[band, at] = jnp.where((t >= begin) & (t <= stop), dual, 0.0)
-
-    last = pltpu.make_async_copy(result_v, dual_demand_o, out_sem.at[len(pairs)])
-    last.start()
+    step = items // PIECES
+    for p in range(PIECES):
+
+        @pl.loop(p * step // LANES, (p + 1) * step // LANES, step=2)
+        def _(i):
+            for j in (i, i + 1):
+                at = pl.ds(pl.multiple_of(j * LANES, LANES), LANES)
+                begin, stop, carry = [
+                    jnp.broadcast_to(window_v[k, pl.ds(j, 1), :], (GROUP, LANES)) for k in range(3)
+                ]
+                for g in range(rows // GROUP):
+                    t = sub + (first + float(g * GROUP))
+                    band = slice(g * GROUP, (g + 1) * GROUP)
+                    dual = jnp.maximum(dual_demand_v[band, at] - dual_step_v[band, at] * carry, 0.0)
+                    result_v[band, at] = jnp.where((t >= begin) & (t <= stop), dual, 0.0)
+
+        at = pl.ds(p * step, step)
+        copies.append(
+            pltpu.make_async_copy(result_v.at[:, at], dual_demand_o.at[:, at], out_sem.at[len(pairs) + p])
+        )
+        copies[-1].start()
+
     for copy in copies:
         copy.wait()
-    last.wait()
 
 
 def shards(ranks, items_total, *args):
@@ -579,14 +622,14 @@
         + [vmem(vector)] * 2
         + [vmem(vector, jnp.int32)] * 3
         + [vmem((blocks, items), BF16)]
-        + [vmem(big)] * 8
+        + [vmem(big)] * 7
         + [
             vmem((2,) + vector),
             vmem((2,) + vector),
             vmem((2, nz, chunks // 2, LANES)),
             vmem((2, nx) + vector),
             vmem((2,) + vector),
-            vmem(vector),
+            vmem((2,) + vector),
             vmem((ny,) + small),
         ]
         + [
@@ -641,7 +684,7 @@
         out_shape=[jax.ShapeDtypeStruct(big, F32)] * 5 + [jax.ShapeDtypeStruct(small, F32)],
         in_specs=[held] * len(between),
         out_specs=[anywhere] * 6,
-        scratch_shapes=[vmem(big), dma((6,))],
+        scratch_shapes=[vmem(big), dma((5 + PIECES,))],
         compiler_params=pltpu.CompilerParams(vmem_limit_bytes=8 * 1024 * 1024),
         name="finish",
     )(*parts)

time: 33.1 us -> 29.9 us (0.903)
  Pallas kernels: 32.3 us -> 29.1 us
    pallas_call x1, Pallas kernels: 30.3 us -> 27.1 us  [shards(): pl.pallas_call(functools.partial(kernel, ranks, items_total), out_shape=[...]
where the time goes in v2:
time: 29.9 us; the launch traced here: 29.7 us
  Pallas kernels  29.1 us (97%)
  between operations  0.65 us (2%)
    pallas_call x1, Pallas kernels, shards(): pl.pallas_call(functools.partial(kernel, ranks, items_total), out_shape=[...  27.1 us
    pallas_call x1, Pallas kernels, shards(): pl.pallas_call(finish, out_shape=[jax.ShapeDtypeStruct(big, F32)] * 5 + [...  2 us

profile of v2, /device:TPU:1, one launch (start us, length us, event | category | flops | bytes accessed | tf_op | source)
XLA Modules:
  0.0 29.7 jit_solution(10446473366474264637)
XLA Ops:
  0.6 27.1 %lot_step.1 = (f32[48,4096]{1,0:T(8,128)S(1)}, f32[48,4096]{1,0:T(8,128)S(1)}, f32[48,4096]{1,0:T(8,128)S(1)}, f32[48,4096]{1,0:T(8,128)S(1)}, f32[48,4096]{1,0:...) custom-call(f32[48,4096]{1,0:T(8,128)} %production_h.1, ...), custom_call_target="tpu_custom_call" | custom-call | tf_op jit(solution)/shard_map/lot_step/pallas_call | solution.py:671
  27.7 2.0 %finish.1 = (f32[48,4096]{1,0:T(8,128)}, f32[48,4096]{1,0:T(8,128)}, f32[48,4096]{1,0:T(8,128)}, f32[48,4096]{1,0:T(8,128)}, f32[48,4096]{1,0:T(8,128)}, /*index=5*/f32[48,128]{1,0:T(8,128)}) custom-call(f32[48,4096]{1,0:T(8,128)S(1)} %get-tuple-element.14.production_v, f32[48,4096]{1,0:T(8,128)S(1)} %get-tuple-element.15.setup_v, ...), custom_call_target="tpu_custom_call" | custom-call | tf_op jit(solution)/shard_map/finish/pallas_call | solution.py:682

commit v3 on v2

--- a/solution.py
+++ b/solution.py
@@ -21,6 +21,7 @@
 CORES = 2
 DEPTH = 8
 UNROLL = 4
+RELAY = 2
 PIECES = 4
 
 
@@ -122,7 +123,8 @@
     along_z_v,
     along_x_v,
     inside_v,
-    carry_v,
+    raw_x_v,
+    column_v,
     usage_v,
     in_sem,
     core_send,
@@ -133,6 +135,9 @@
     x_recv,
     inside_send,
     inside_recv,
+    raw_send,
+    raw_recv,
+    ready,
     y_send,
     y_recv,
 ):
@@ -153,7 +158,7 @@
 
     barrier = pltpu.get_barrier_semaphore()
     greeted = 0
-    for d in far_first(nz):
+    for d in [d for d in far_first(nz) if min(d, nz - d) <= RELAY]:
         pl.semaphore_signal(
             barrier, inc=1, device_id=place(x, lax.rem(z + d, nz), core), device_id_type=MESH
         )
@@ -239,118 +244,184 @@
 
     pl.semaphore_wait(barrier, greeted)
 
-    sent = []
-
     def remote(src, dst, send, recv, where):
         return pltpu.make_async_remote_copy(
             src_ref=src, dst_ref=dst, send_sem=send, recv_sem=recv, device_id=where, device_id_type=MESH
         )
 
-    mine = pl.ds(pl.multiple_of(core * half, half), half)
-    other = pl.ds(pl.multiple_of((1 - core) * half, half), half)
+    def part(h):
+        return pl.ds(pl.multiple_of(h * half, half), half)
 
     sibling = place(x, z, 1 - core)
+    mine, other = part(core), part(1 - core)
 
     def halfway(s, h):
-        part = pl.ds(pl.multiple_of(h * half, half), half)
         return remote(
-            own_v.at[s, part], sibling_v.at[s, part], core_send.at[s, h], core_recv.at[s, h], sibling
-        )
-
-    def hand_over(s, h):
-        copy = halfway(s, h)
-        copy.start()
-        sent.append(copy)
-
-    def across(s, d, c):
+            own_v.at[s, part(h)], sibling_v.at[s, part(h)], core_send.at[s, h], core_recv.at[s, h], sibling
+        )
+
+    def along(s, src, e):
         return remote(
-            along_x_v.at[s, x, mine],
-            along_x_v.at[s, x, mine],
-            x_send.at[s, d, c],
-            x_recv.at[s, x, core],
+            src, along_z_v.at[s, z], z_send.at[s, e], z_recv.at[s, z], place(x, lax.rem(z + e, nz), core)
+        )
+
+    def from_along(s, e):
+        there = lax.rem(z + e, nz)
+        remote(
+            along_z_v.at[s, there],
+            along_z_v.at[s, there],
+            z_send.at[s, e],
+            z_recv.at[s, there],
+            place(x, there, core),
+        ).wait_recv()
+        return along_z_v[s, there]
+
+    def raw(d, c):
+        return remote(
+            own_v.at[0, part(c)],
+            raw_x_v.at[x, core],
+            raw_send.at[d, c],
+            raw_recv.at[x, core],
             place(lax.rem(x + d, nx), z, c),
         )
 
-    def carried(s, later, during_z, during_x):
-        def counts(there, here):
-            return there > here if later else there < here
-
-        halfway(s, core).wait_recv()
-        along_z_v[s, z] = own_v[s, mine, :] + sibling_v[s, mine, :]
-        for d in far_first(nz):
-            copy = remote(
-                along_z_v.at[s, z],
-                along_z_v.at[s, z],
-                z_send.at[s, d],
-                z_recv.at[s, z],
-                place(x, lax.rem(z + d, nz), core),
-            )
-            copy.start()
-            sent.append(copy)
-        during_z()
-        for d in range(1, nz):
-            there = lax.rem(z + d, nz)
-            remote(
-                along_z_v.at[s, there],
-                along_z_v.at[s, there],
-                z_send.at[s, d],
-                z_recv.at[s, there],
-                place(x, there, core),
-            ).wait_recv()
-        whole = along_z_v[s, 0]
-        partial = jnp.where(counts(0, z), whole, 0.0)
-        for k in range(1, nz):
-            term = along_z_v[s, k]
-            whole = whole + term
-            partial = partial + jnp.where(counts(k, z), term, 0.0)
-        along_x_v[s, x, mine, :] = whole
-        inside_v[s, mine, :] = partial
+    def across(d, c):
+        return remote(
+            along_x_v.at[x, other],
+            along_x_v.at[x, other],
+            x_send.at[d, c],
+            x_recv.at[x, 1 - core],
+            place(lax.rem(x + d, nx), z, c),
+        )
+
+    def inside(s, where):
+        return remote(
+            inside_v.at[s, where], inside_v.at[s, where], inside_send.at[s], inside_recv.at[s], sibling
+        )
+
+    def column(e):
+        there = lax.rem(z + e, nz)
+        return along(0, column_v.at[jnp.where(z > there, 1, 0)], e)
+
+    later_core = core == 0
+
+    def suffix_scan(during_x, during_z):
         for d in far_first(nx):
-            there = lax.rem(x + d, nx)
-
-            @pl.when(counts(x, there))
+
+            @pl.when(x > lax.rem(x + d, nx))
             def _():
                 for c in range(CORES):
-                    across(s, d, c).start()
-
-        to_core = remote(
-            inside_v.at[s, mine], inside_v.at[s, mine], inside_send.at[s], inside_recv.at[s], sibling
-        )
-        to_core.start()
-        sent.append(to_core)
+                    raw(d, c).start()
+
+        halfway(0, 1 - core).start()
+        halfway(0, core).start()
+        for e in (RELAY, nz - RELAY):
+            pl.semaphore_signal(
+                ready, inc=1, device_id=place(x, lax.rem(z + e, nz), core), device_id_type=MESH
+            )
         during_x()
-        halfway(s, 1 - core).wait_recv()
-        remote(
-            inside_v.at[s, other], inside_v.at[s, other], inside_send.at[s], inside_recv.at[s], sibling
-        ).wait_recv()
-        carry_v[s] = inside_v[s] + jnp.where(counts(1 - core, core), sibling_v[s], 0.0)
+        halfway(0, core).wait_recv()
+        column_v[0] = jnp.zeros((half, LANES), F32)
         for d in reversed(far_first(nx)):
             there = lax.rem(x + d, nx)
 
-            @pl.when(counts(there, x))
+            @pl.when(there > x)
             def _():
                 for c in range(CORES):
-                    part = pl.ds(c * half, half)
                     remote(
-                        along_x_v.at[s, there, part],
-                        along_x_v.at[s, there, part],
-                        x_send.at[s, d, c],
-                        x_recv.at[s, there, c],
+                        raw_x_v.at[there, c],
+                        raw_x_v.at[there, c],
+                        raw_send.at[d, c],
+                        raw_recv.at[there, c],
                         place(there, z, c),
                     ).wait_recv()
-                carry_v[s] += along_x_v[s, there]
-
-    def left(s, later):
-        for copy in sent:
-            copy.wait_send()
-        sent.clear()
+                column_v[0] += raw_x_v[there, 0] + raw_x_v[there, 1]
+
+        column_v[1] = column_v[0] + (own_v[0, mine, :] + sibling_v[0, mine, :])
+        pl.semaphore_wait(ready, 2)
+        for e in far_first(nz):
+            column(e).start()
+        during_z()
+        total = column_v[0]
+        for e in reversed(far_first(nz)):
+            total = total + from_along(0, e)
+        inside_v[0, mine, :] = total
+        inside(0, mine).start()
+        window_v[2, mine, :] = total + jnp.where(later_core, sibling_v[0, mine, :], 0.0)
+
+    def suffix_other():
+        halfway(0, 1 - core).wait_recv()
+        inside(0, other).wait_recv()
+        window_v[2, other, :] = inside_v[0, other, :] + jnp.where(
+            later_core, sibling_v[0, other, :], 0.0
+        )
+
+    def suffix_left():
         for d in far_first(nx):
-            there = lax.rem(x + d, nx)
-
-            @pl.when(x > there if later else x < there)
+
+            @pl.when(x > lax.rem(x + d, nx))
             def _():
                 for c in range(CORES):
-                    across(s, d, c).wait_send()
+                    raw(d, c).wait_send()
+
+        for h in range(CORES):
+            halfway(0, h).wait_send()
+        for e in far_first(nz):
+            column(e).wait_send()
+        inside(0, mine).wait_send()
+
+    def prefix_scan(during_z, during_x):
+        halfway(1, 1 - core).wait_recv()
+        along_z_v[1, z] = own_v[1, other, :] + sibling_v[1, other, :]
+        for e in far_first(nz):
+            along(1, along_z_v.at[1, z], e).start()
+        during_z()
+        whole = along_z_v[1, z]
+        partial = jnp.zeros_like(whole)
+        for e in reversed(far_first(nz)):
+            term = from_along(1, e)
+            whole = whole + term
+            partial = partial + jnp.where(lax.rem(z + e, nz) < z, term, 0.0)
+        along_x_v[x, other, :] = whole
+        for d in far_first(nx):
+
+            @pl.when(x < lax.rem(x + d, nx))
+            def _():
+                for c in range(CORES):
+                    across(d, c).start()
+
+        inside_v[1, other, :] = partial
+        inside(1, other).start()
+        during_x()
+        halfway(1, core).wait_recv()
+        inside(1, mine).wait_recv()
+        window_v[3] = inside_v[1] + jnp.where(later_core, 0.0, sibling_v[1])
+        for d in reversed(far_first(nx)):
+            there = lax.rem(x + d, nx)
+
+            @pl.when(there < x)
+            def _():
+                for h in range(CORES):
+                    remote(
+                        along_x_v.at[there, part(h)],
+                        along_x_v.at[there, part(h)],
+                        x_send.at[d, h],
+                        x_recv.at[there, h],
+                        place(there, z, h),
+                    ).wait_recv()
+                window_v[3] += along_x_v[there]
+
+        for h in range(CORES):
+            halfway(1, h).wait_send()
+        for e in far_first(nz):
+            along(1, along_z_v.at[1, z], e).wait_send()
+        inside(1, other).wait_send()
+        for d in far_first(nx):
+
+            @pl.when(x < lax.rem(x + d, nx))
+            def _():
+                for c in range(CORES):
+                    across(d, c).wait_send()
 
     def pull():
         arrived("block", "dual_resource", "coef_production", "coef_setup")
@@ -376,6 +447,19 @@
             pull_setup_v[:, at] = pulled[3 * rows : 4 * rows] + (
                 pulled[4 * rows : 5 * rows] + pulled[5 * rows : 6 * rows]
             )
+
+    def used(bar_v, coef_v):
+        deep = DEPTH * LANES
+
+        def add_blocks(i, total):
+            at = pl.ds(pl.multiple_of(i * deep, deep), deep)
+            left = jnp.concatenate(halves(bar_v[:, at], 2), axis=0)
+            return total + lax.dot_general(
+                left, onehot_v[:, at], (((1,), (1,)), ((), ())), preferred_element_type=F32
+            )
+
+        by_block = lax.fori_loop(0, items // deep, add_blocks, jnp.zeros((2 * rows, blocks), F32))
+        return exact(by_block[0:rows] + by_block[rows : 2 * rows], coef_v[...], ((1,), (0,)))
 
     def own_part():
         arrived(
@@ -429,15 +513,16 @@
                 put(shortage_v, g, j, late)
                 put(dual_demand_v, g, j, dual_active - dual_step * (2.0 * late - before))
 
-    hand_over(0, 1 - core)
-    hand_over(0, core)
-    carried(0, True, pull, own_part)
-
+    def own_and_usage():
+        own_part()
+        usage_v[y] = used(setup_bar_v, coef_setup_v)
+
+    suffix_scan(pull, own_and_usage)
     arrived("demand")
 
     def net_production(j):
         begin, stop, active = window(j)
-        carry = row(carry_v.at[0], j)
+        carry = row(window_v.at[2], j)
         total = jnp.zeros((GROUP, LANES), F32)
         for g in range(groups):
             on = active[g]
@@ -450,16 +535,28 @@
             total = total + (bar - jnp.where(on, piece(demand_v, g, j), 0.0))
         own_v[1, pl.ds(j, 1), :] = jnp.sum(total, axis=0, keepdims=True)
 
-    for h in (1 - core, core):
-
+    def net_half(h):
         @pl.loop(0, half // UNROLL)
         def _(i):
             for k in range(UNROLL):
                 net_production(h * half + i * UNROLL + k)
 
-        hand_over(1, h)
+        halfway(1, h).start()
+
+    net_half(core)
+    suffix_other()
+    net_half(1 - core)
+
+    def beside(d):
+        return remote(
+            usage_v.at[y], usage_v.at[y], y_send.at[d], y_recv.at[y], place(x, z, core, lax.rem(y + d, ny))
+        )
 
     def dual_part():
+        usage_v[y] += used(prod_bar_v, coef_production_v)
+        for d in range(1, ny):
+            beside(d).start()
+
         @pl.loop(0, chunks)
         def _(j):
             begin, stop, active = window(j)
@@ -478,30 +575,9 @@
                 link = jnp.maximum(piece(link_v, g, j) + link_step * piece(prod_bar_v, g, j), 0.0)
                 put(dual_link_v, g, j, jnp.where(active[g], link, 0.0))
 
-        deep = DEPTH * LANES
-
-        def add_blocks(i, total):
-            at = pl.ds(pl.multiple_of(i * deep, deep), deep)
-            terms = halves(prod_bar_v[:, at], 2) + halves(setup_bar_v[:, at], 2)
-            left = jnp.concatenate(terms, axis=0)
-            return total + lax.dot_general(
-                left, onehot_v[:, at], (((1,), (1,)), ((), ())), preferred_element_type=F32
-            )
-
-        by_block = lax.fori_loop(0, items // deep, add_blocks, jnp.zeros((4 * rows, blocks), F32))
-        usage_v[y] = exact(
-            by_block[0:rows] + by_block[rows : 2 * rows], coef_production_v[...], ((1,), (0,))
-        ) + exact(
-            by_block[2 * rows : 3 * rows] + by_block[3 * rows : 4 * rows], coef_setup_v[...], ((1,), (0,))
-        )
+    def resource_part():
         for d in range(1, ny):
-            copy = remote(
-                usage_v.at[y], usage_v.at[y], y_send.at[d], y_recv.at[y], place(x, z, core, lax.rem(y + d, ny))
-            )
-            copy.start()
-            sent.append(copy)
-
-    def resource_part():
+            beside(d).wait_send()
         for d in range(1, ny):
             there = lax.rem(y + d, ny)
             remote(
@@ -514,13 +590,8 @@
         scale = dual_resource_v.shape[1] / items_total
         dual_resource_v[...] = jnp.maximum(dual_resource_v[...] + scale * (usage - capacity_v[...]), 0.0)
 
-    def rest():
-        resource_part()
-        left(0, True)
-
-    carried(1, False, dual_part, rest)
-    window_v[2] = carry_v[1]
-    left(1, False)
+    prefix_scan(dual_part, suffix_left)
+    resource_part()
 
 
 def finish(
@@ -563,7 +634,7 @@
             for j in (i, i + 1):
                 at = pl.ds(pl.multiple_of(j * LANES, LANES), LANES)
                 begin, stop, carry = [
-                    jnp.broadcast_to(window_v[k, pl.ds(j, 1), :], (GROUP, LANES)) for k in range(3)
+                    jnp.broadcast_to(window_v[k, pl.ds(j, 1), :], (GROUP, LANES)) for k in (0, 1, 3)
                 ]
                 for g in range(rows // GROUP):
                     t = sub + (first + float(g * GROUP))
@@ -627,9 +698,10 @@
             vmem((2,) + vector),
             vmem((2,) + vector),
             vmem((2, nz, chunks // 2, LANES)),
-            vmem((2, nx) + vector),
+            vmem((nx,) + vector),
             vmem((2,) + vector),
-            vmem((2,) + vector),
+            vmem((nx, CORES, chunks // 2, LANES)),
+            vmem((2, chunks // 2, LANES)),
             vmem((ny,) + small),
         ]
         + [
@@ -638,10 +710,13 @@
             dma((2, CORES)),
             dma((2, nz)),
             dma((2, nz)),
-            dma((2, nx, CORES)),
-            dma((2, nx, CORES)),
+            dma((nx, CORES)),
+            dma((nx, CORES)),
             dma((2,)),
             dma((2,)),
+            dma((nx, CORES)),
+            dma((nx, CORES)),
+            pltpu.SemaphoreType.REGULAR,
             dma((ny,)),
             dma((ny,)),
         ]
@@ -667,7 +742,7 @@
     ]
     operands = [pltpu.with_memory_space_constraint(a, pltpu.HBM) for a in operands]
     held = pl.BlockSpec(memory_space=pltpu.VMEM)
-    between = [big] * 5 + [small, big, (3,) + vector]
+    between = [big] * 5 + [small, big, (4,) + vector]
     parts = pl.pallas_call(
         functools.partial(kernel, ranks, items_total),
         out_shape=[pltpu.VMEM(shape, F32) for shape in between],

time: 29.9 us -> 28.2 us (0.943)
  Pallas kernels: 29.1 us -> 27.4 us
    pallas_call x1, Pallas kernels: 27.1 us -> 25.4 us  [shards(): pl.pallas_call(functools.partial(kernel, ranks, items_total), out_shape=[...]
where the time goes in v3:
time: 28.2 us; the launch traced here: 28 us
  Pallas kernels  27.4 us (97%)
  between operations  0.65 us (2%)
    pallas_call x1, Pallas kernels, shards(): pl.pallas_call(functools.partial(kernel, ranks, items_total), out_shape=[...  25.4 us
    pallas_call x1, Pallas kernels, shards(): pl.pallas_call(finish, out_shape=[jax.ShapeDtypeStruct(big, F32)] * 5 + [...  2 us

profile of v3, /device:TPU:1, one launch (start us, length us, event | category | flops | bytes accessed | tf_op | source)
XLA Modules:
  0.0 28.0 jit_solution(13792490657548753093)
XLA Ops:
  0.6 25.4 %lot_step.1 = (f32[48,4096]{1,0:T(8,128)S(1)}, f32[48,4096]{1,0:T(8,128)S(1)}, f32[48,4096]{1,0:T(8,128)S(1)}, f32[48,4096]{1,0:T(8,128)S(1)}, f32[48,4096]{1,0:...) custom-call(f32[48,4096]{1,0:T(8,128)} %production_h.1, ...), custom_call_target="tpu_custom_call" | custom-call | tf_op jit(solution)/shard_map/lot_step/pallas_call | solution.py:746
  26.0 2.0 %finish.1 = (f32[48,4096]{1,0:T(8,128)}, f32[48,4096]{1,0:T(8,128)}, f32[48,4096]{1,0:T(8,128)}, f32[48,4096]{1,0:T(8,128)}, f32[48,4096]{1,0:T(8,128)}, /*index=5*/f32[48,128]{1,0:T(8,128)}) custom-call(f32[48,4096]{1,0:T(8,128)S(1)} %get-tuple-element.14.production_v, f32[48,4096]{1,0:T(8,128)S(1)} %get-tuple-element.15.setup_v, ...), custom_call_target="tpu_custom_call" | custom-call | tf_op jit(solution)/shard_map/finish/pallas_call | solution.py:757

commit v4 on v3

--- a/solution.py
+++ b/solution.py
@@ -19,10 +19,10 @@
 LANES = 128
 GROUP = 8
 CORES = 2
-DEPTH = 8
-UNROLL = 4
+DEPTH = 16
+UNROLL = 16
 RELAY = 2
-PIECES = 4
+PIECES = 2
 
 
 def suffix_rows(groups, sub):
@@ -115,6 +115,8 @@
     pull_setup_v,
     local_v,
     primal_step_v,
+    given_v,
+    fixed_v,
     setup_bar_v,
     prod_bar_v,
     link_v,
@@ -191,7 +193,7 @@
         "setup": (setup_h, setup_v),
         "fixing": (fixing_h, fixing_v),
         "shortage": (shortage_h, shortage_v),
-        "production": (production_h, production_v),
+        "production": (production_h, given_v),
         "cost_production": (cost_production_h, cost_production_v),
         "demand": (demand_h, demand_v),
         "capacity": (capacity_h, capacity_v),
@@ -382,6 +384,8 @@
             term = from_along(1, e)
             whole = whole + term
             partial = partial + jnp.where(lax.rem(z + e, nz) < z, term, 0.0)
+        inside_v[1, other, :] = partial
+        inside(1, other).start()
         along_x_v[x, other, :] = whole
         for d in far_first(nx):
 
@@ -390,11 +394,13 @@
                 for c in range(CORES):
                     across(d, c).start()
 
-        inside_v[1, other, :] = partial
-        inside(1, other).start()
         during_x()
         halfway(1, core).wait_recv()
         inside(1, mine).wait_recv()
+        for h in range(CORES):
+            halfway(1, h).wait_send()
+        for e in far_first(nz):
+            along(1, along_z_v.at[1, z], e).wait_send()
         window_v[3] = inside_v[1] + jnp.where(later_core, 0.0, sibling_v[1])
         for d in reversed(far_first(nx)):
             there = lax.rem(x + d, nx)
@@ -411,10 +417,6 @@
                     ).wait_recv()
                 window_v[3] += along_x_v[there]
 
-        for h in range(CORES):
-            halfway(1, h).wait_send()
-        for e in far_first(nz):
-            along(1, along_z_v.at[1, z], e).wait_send()
         inside(1, other).wait_send()
         for d in far_first(nx):
 
@@ -422,6 +424,8 @@
             def _():
                 for c in range(CORES):
                     across(d, c).wait_send()
+
+    wide = 4
 
     def pull():
         arrived("block", "dual_resource", "coef_production", "coef_setup")
@@ -430,7 +434,6 @@
         stacked = jnp.concatenate(
             [t.astype(F32) for t in halves(by_block_production, 3) + halves(by_block_setup, 3)], axis=0
         ).astype(BF16)
-        wide = 4
 
         @pl.loop(0, chunks // wide)
         def _(i):
@@ -471,6 +474,7 @@
             "shortage",
             "production",
             "cost_production",
+            "demand",
         )
 
         @pl.loop(0, chunks)
@@ -478,6 +482,7 @@
             begin, stop, active = window(j)
             setup_price = row(cost_setup_v, j)
             late_price = row(penalty_v, j)
+            fixed = jnp.zeros((GROUP, LANES), F32)
             for g in range(groups):
                 on = active[g]
                 dual_active = jnp.where(on, piece(dual_demand_v, g, j), 0.0)
@@ -490,8 +495,10 @@
                     + link_active
                     + piece(pull_production_v, g, j)
                 )
-                put(local_v, g, j, piece(production_v, g, j) - primal_step * price)
-                put(primal_step_v, g, j, primal_step)
+                before = piece(given_v, g, j)
+                put(local_v, g, j, jnp.where(on, before - primal_step * price, 0.0))
+                put(primal_step_v, g, j, jnp.where(on, primal_step, 0.0))
+                fixed = fixed + jnp.where(on, before + piece(demand_v, g, j), 0.0)
                 put(dual_step_v, g, j, dual_step)
                 before = piece(setup_v, g, j)
                 moved = jnp.clip(
@@ -512,28 +519,23 @@
                 )
                 put(shortage_v, g, j, late)
                 put(dual_demand_v, g, j, dual_active - dual_step * (2.0 * late - before))
+            fixed_v[pl.ds(j, 1), :] = jnp.sum(fixed, axis=0, keepdims=True)
 
     def own_and_usage():
         own_part()
         usage_v[y] = used(setup_bar_v, coef_setup_v)
 
     suffix_scan(pull, own_and_usage)
-    arrived("demand")
-
     def net_production(j):
-        begin, stop, active = window(j)
         carry = row(window_v.at[2], j)
         total = jnp.zeros((GROUP, LANES), F32)
         for g in range(groups):
-            on = active[g]
-            before = piece(production_v, g, j)
             made = jnp.maximum(piece(local_v, g, j) + piece(primal_step_v, g, j) * carry, 0.0)
-            made = jnp.where(on, made, 0.0)
             put(production_v, g, j, made)
-            bar = jnp.where(on, 2.0 * made - before, 0.0)
-            put(prod_bar_v, g, j, bar)
-            total = total + (bar - jnp.where(on, piece(demand_v, g, j), 0.0))
-        own_v[1, pl.ds(j, 1), :] = jnp.sum(total, axis=0, keepdims=True)
+            total = total + made
+        own_v[1, pl.ds(j, 1), :] = (
+            2.0 * jnp.sum(total, axis=0, keepdims=True) - fixed_v[pl.ds(j, 1), :]
+        )
 
     def net_half(h):
         @pl.loop(0, half // UNROLL)
@@ -553,6 +555,15 @@
         )
 
     def dual_part():
+        @pl.loop(0, chunks // wide)
+        def _(i):
+            for k in range(wide):
+                j = i * wide + k
+                begin, stop, active = window(j)
+                for g in range(groups):
+                    bar = 2.0 * piece(production_v, g, j) - piece(given_v, g, j)
+                    put(prod_bar_v, g, j, jnp.where(active[g], bar, 0.0))
+
         usage_v[y] += used(prod_bar_v, coef_production_v)
         for d in range(1, ny):
             beside(d).start()
@@ -590,8 +601,11 @@
         scale = dual_resource_v.shape[1] / items_total
         dual_resource_v[...] = jnp.maximum(dual_resource_v[...] + scale * (usage - capacity_v[...]), 0.0)
 
-    prefix_scan(dual_part, suffix_left)
-    resource_part()
+    def dual_and_left():
+        dual_part()
+        suffix_left()
+
+    prefix_scan(dual_and_left, resource_part)
 
 
 def finish(
@@ -693,7 +707,9 @@
         + [vmem(vector)] * 2
         + [vmem(vector, jnp.int32)] * 3
         + [vmem((blocks, items), BF16)]
-        + [vmem(big)] * 7
+        + [vmem(big)] * 5
+        + [vmem(vector)]
+        + [vmem(big)] * 3
         + [
             vmem((2,) + vector),
             vmem((2,) + vector),

time: 28.2 us -> 27.9 us (0.989)
  Pallas kernels: 27.4 us -> 27.1 us
    pallas_call x1, Pallas kernels: 25.4 us -> 25.1 us  [shards(): pl.pallas_call(functools.partial(kernel, ranks, items_total), out_shape=[...]
where the time goes in v4:
time: 27.9 us; the launch traced here: 27.7 us
  Pallas kernels  27.1 us (97%)
  between operations  0.65 us (2%)
    pallas_call x1, Pallas kernels, shards(): pl.pallas_call(functools.partial(kernel, ranks, items_total), out_shape=[...  25.1 us
    pallas_call x1, Pallas kernels, shards(): pl.pallas_call(finish, out_shape=[jax.ShapeDtypeStruct(big, F32)] * 5 + [...  1.98 us

profile of v4, /device:TPU:1, one launch (start us, length us, event | category | flops | bytes accessed | tf_op | source)
XLA Modules:
  0.0 27.7 jit_solution(14837342548630951353)
XLA Ops:
  0.6 25.1 %lot_step.1 = (f32[48,4096]{1,0:T(8,128)S(1)}, f32[48,4096]{1,0:T(8,128)S(1)}, f32[48,4096]{1,0:T(8,128)S(1)}, f32[48,4096]{1,0:T(8,128)S(1)}, f32[48,4096]{1,0:...) custom-call(f32[48,4096]{1,0:T(8,128)} %production_h.1, ...), custom_call_target="tpu_custom_call" | custom-call | tf_op jit(solution)/shard_map/lot_step/pallas_call | solution.py:762
  25.7 2.0 %finish.1 = (f32[48,4096]{1,0:T(8,128)}, f32[48,4096]{1,0:T(8,128)}, f32[48,4096]{1,0:T(8,128)}, f32[48,4096]{1,0:T(8,128)}, f32[48,4096]{1,0:T(8,128)}, /*index=5*/f32[48,128]{1,0:T(8,128)}) custom-call(f32[48,4096]{1,0:T(8,128)S(1)} %get-tuple-element.14.production_v, f32[48,4096]{1,0:T(8,128)S(1)} %get-tuple-element.15.setup_v, ...), custom_call_target="tpu_custom_call" | custom-call | tf_op jit(solution)/shard_map/finish/pallas_call | solution.py:773

commit v5 on v4

--- a/solution.py
+++ b/solution.py
@@ -159,25 +159,17 @@
         return ((px * nz + pz) * CORES + pc, y if py is None else py)
 
     barrier = pltpu.get_barrier_semaphore()
-    greeted = 0
-    for d in [d for d in far_first(nz) if min(d, nz - d) <= RELAY]:
-        pl.semaphore_signal(
-            barrier, inc=1, device_id=place(x, lax.rem(z + d, nz), core), device_id_type=MESH
-        )
-        greeted += 1
-    for d in far_first(nx):
+    greetings = [(min(d, nz - d), place(x, lax.rem(z + d, nz), core)) for d in range(1, nz)]
+    greetings = [(far, where) for far, where in greetings if far <= RELAY]
+    for d in range(1, nx):
         for c in range(CORES):
-            pl.semaphore_signal(
-                barrier, inc=1, device_id=place(lax.rem(x + d, nx), z, c), device_id_type=MESH
-            )
-            greeted += 1
+            greetings.append((min(d, nx - d), place(lax.rem(x + d, nx), z, c)))
     for d in range(1, ny):
-        pl.semaphore_signal(
-            barrier, inc=1, device_id=place(x, z, core, lax.rem(y + d, ny)), device_id_type=MESH
-        )
-        greeted += 1
-    pl.semaphore_signal(barrier, inc=1, device_id=place(x, z, 1 - core), device_id_type=MESH)
-    greeted += 1
+        greetings.append((min(d, ny - d), place(x, z, core, lax.rem(y + d, ny))))
+    greetings.append((0, place(x, z, 1 - core)))
+    for _, where in sorted(greetings, key=lambda item: -item[0]):
+        pl.semaphore_signal(barrier, inc=1, device_id=where, device_id_type=MESH)
+    greeted = len(greetings)
 
     loads = {
         "start": (start_h, start_v),

time: 27.9 us -> 27.9 us (level)
  no operation moved by 1% of the time
where the time goes in v5:
time: 27.9 us; the launch traced here: 27.7 us
  Pallas kernels  27 us (97%)
  between operations  0.65 us (2%)
    pallas_call x1, Pallas kernels, shards(): pl.pallas_call(functools.partial(kernel, ranks, items_total), out_shape=[...  25.1 us
    pallas_call x1, Pallas kernels, shards(): pl.pallas_call(finish, out_shape=[jax.ShapeDtypeStruct(big, F32)] * 5 + [...  1.98 us

profile of v5, /device:TPU:1, one launch (start us, length us, event | category | flops | bytes accessed | tf_op | source)
XLA Modules:
  0.0 27.7 jit_solution(10394543749264721768)
XLA Ops:
  0.6 25.1 %lot_step.1 = (f32[48,4096]{1,0:T(8,128)S(1)}, f32[48,4096]{1,0:T(8,128)S(1)}, f32[48,4096]{1,0:T(8,128)S(1)}, f32[48,4096]{1,0:T(8,128)S(1)}, f32[48,4096]{1,0:...) custom-call(f32[48,4096]{1,0:T(8,128)} %production_h.1, ...), custom_call_target="tpu_custom_call" | custom-call | tf_op jit(solution)/shard_map/lot_step/pallas_call | solution.py:754
  25.7 2.0 %finish.1 = (f32[48,4096]{1,0:T(8,128)}, f32[48,4096]{1,0:T(8,128)}, f32[48,4096]{1,0:T(8,128)}, f32[48,4096]{1,0:T(8,128)}, f32[48,4096]{1,0:T(8,128)}, /*index=5*/f32[48,128]{1,0:T(8,128)}) custom-call(f32[48,4096]{1,0:T(8,128)S(1)} %get-tuple-element.14.production_v, f32[48,4096]{1,0:T(8,128)S(1)} %get-tuple-element.15.setup_v, ...), custom_call_target="tpu_custom_call" | custom-call | tf_op jit(solution)/shard_map/finish/pallas_call | solution.py:765
